TPU v7x, 32 devices: a whole 2x2x4 slice. The times are simulated.
32 devices in a mesh: section: 2 (over core), ctx: 16 (over z, y, x).
Axes of the slice: x: 2, y: 2, z: 4, core: 2. Of those that a mesh axis runs over, the one named last changes fastest.
Arguments:
- queries: bfloat16 [2, 2048, 2560], P('section', 'ctx'), may hold values from -6 to 6
- keys: bfloat16 [2048, 512], P('ctx'), may hold values from -6 to 6
- values: bfloat16 [2048, 512], P('ctx'), may hold values from -6 to 6
- cotangent: bfloat16 [2, 2048, 2560], P('section', 'ctx'), may hold values from -6 to 6
- segment_ids: int32 [2048], P('ctx'), may hold values from 0 to 23, never falling along the last dimension, each value on 1 to 256 neighbouring positions
Outputs:
- grad_queries: bfloat16 [2, 2048, 2560], P('section', 'ctx')
- grad_keys: float32 [2048, 512], P('ctx', 'section')
- grad_values: float32 [2048, 512], P('ctx', 'section')
Inputs may be any that keep to these rules, and one draw needn't show every extreme that they name: `segment_ids`: ids never fall; each document covers 1 to 256 tokens, one exactly 256.
All inputs are finite; a program needn't handle non-finite values.
Results may differ from a plain program's by a relative error of at most 0.007.
Values may be sent and summed in bfloat16 or wider, within the bound.
A program may use at most 64 MiB of HBM per device.

v0:
```python
import jax
import jax.numpy as jnp
from jax import lax
from jax.sharding import PartitionSpec as P

DH = 128
DOC_SHARDS = 2


def shifted(shard, axis, by):
    size = lax.axis_size(axis)
    pairs = [(i, i + by) for i in range(size) if 0 <= i + by < size]
    return lax.ppermute(shard, axis, pairs)


def as_sent(shard):

    def short(part):
        return part.astype(jnp.bfloat16) if part.dtype == jnp.float32 else part

    return jax.tree.map(short, shard)


def by_group(rows, groups):
    count, width = rows.shape
    head_ratio = width // (groups * DH)
    return (
        rows.reshape(count, groups, head_ratio, DH)
        .transpose(1, 2, 0, 3)
        .reshape(groups, head_ratio * count, DH)
    )


def add_pair(first, second):
    return (first[0] + second[0], first[1] + second[1])


def on_device(queries, keys, values, cotangent, segment_ids):
    tok_rows = keys.shape[0]
    groups = keys.shape[1] // DH
    heads = queries.shape[2] // DH
    head_ratio = heads // groups
    score_scale = DH ** (-0.5)
    cycle_size = lax.axis_size("ctx")
    my_index = lax.axis_index("ctx")
    query_rows = by_group(queries[0], groups)
    grad_rows = by_group(cotangent[0], groups)
    row_pos = my_index * tok_rows + jnp.tile(jnp.arange(tok_rows, dtype=jnp.int32), head_ratio)
    row_seg = jnp.tile(segment_ids, head_ratio)
    blocks = []
    current = (keys, values, segment_ids)
    for shard_step in range(DOC_SHARDS + 1):
        if shard_step > 0:
            current = shifted((current[0], current[1], current[2]), "ctx", 1)
        key_block, value_block, key_seg = current
        key_rows = key_block.reshape(tok_rows, groups, DH).transpose(1, 0, 2)
        value_rows = value_block.reshape(tok_rows, groups, DH).transpose(1, 0, 2)
        key_pos = (my_index - shard_step) % cycle_size * tok_rows + jnp.arange(
            tok_rows, dtype=jnp.int32
        )
        allowed = (row_seg[:, None] == key_seg[None, :]) & (key_pos[None, :] <= row_pos[:, None])
        if shard_step == 0:
            is_live = jnp.array(True)
        else:
            is_live = (my_index >= shard_step) & (key_seg[-1] >= segment_ids[0])
        blocks.append((key_rows, value_rows, allowed, is_live))
    row_count = head_ratio * tok_rows
    row_max = jnp.full((groups, row_count, 1), -1e30, jnp.float32)
    row_sum = jnp.zeros((groups, row_count, 1), jnp.float32)
    kept_scores = []
    for key_rows, value_rows, allowed, is_live in blocks:

        def running_stats(key_rows=key_rows, allowed=allowed, row_max=row_max, row_sum=row_sum):
            scores = (
                jnp.einsum("grd,gkd->grk", query_rows, key_rows, preferred_element_type=jnp.float32)
                * score_scale
            )
            block_max = jnp.max(jnp.where(allowed, scores, -1e30), -1, keepdims=True)
            new_max = jnp.maximum(row_max, block_max)
            added = jnp.sum(jnp.where(allowed, jnp.exp(scores - new_max), 0.0), -1, keepdims=True)
            return (new_max, row_sum * jnp.exp(row_max - new_max) + added, scores)

        row_max, row_sum, scores = running_stats()
        kept_scores.append(scores)
    log_total = row_max + jnp.log(row_sum)

    def block_probs(scores, allowed):
        return jnp.where(allowed, jnp.exp(scores - log_total), 0.0)

    output_rows = jnp.zeros((groups, row_count, DH), jnp.float32)
    for (key_rows, value_rows, allowed, is_live), scores in zip(blocks, kept_scores):

        def output_part(scores=scores, value_rows=value_rows, allowed=allowed):
            probs_low = block_probs(scores, allowed).astype(jnp.bfloat16)
            return jnp.einsum(
                "grk,gkd->grd", probs_low, value_rows, preferred_element_type=jnp.float32
            )

        output_rows = output_rows + output_part()
    row_dot = jnp.sum(grad_rows.astype(jnp.float32) * output_rows, -1, keepdims=True)
    grad_query = jnp.zeros((groups, row_count, DH), jnp.float32)
    partials = []
    for (key_rows, value_rows, allowed, is_live), scores in zip(blocks, kept_scores):

        def backward_part(scores=scores, key_rows=key_rows, value_rows=value_rows, allowed=allowed):
            probs = block_probs(scores, allowed)
            probs_low = probs.astype(jnp.bfloat16)
            grad_probs = jnp.einsum(
                "grd,gkd->grk", grad_rows, value_rows, preferred_element_type=jnp.float32
            )
            scaled_low = (probs * (grad_probs - row_dot) * score_scale).astype(jnp.bfloat16)
            query_part = jnp.einsum(
                "grk,gkd->grd", scaled_low, key_rows, preferred_element_type=jnp.float32
            )
            key_part = jnp.einsum(
                "grk,grd->gkd", scaled_low, query_rows, preferred_element_type=jnp.float32
            )
            value_part = jnp.einsum(
                "grk,grd->gkd", probs_low, grad_rows, preferred_element_type=jnp.float32
            )
            key_flat = key_part.transpose(1, 0, 2).reshape(tok_rows, groups * DH)
            value_flat = value_part.transpose(1, 0, 2).reshape(tok_rows, groups * DH)
            return (query_part, key_flat, value_flat)

        query_part, key_flat, value_flat = backward_part()
        grad_query = grad_query + query_part
        partials.append((key_flat, value_flat))
    summed = partials[0]
    for shard_step in range(1, DOC_SHARDS + 1):
        arrived = shifted(as_sent(partials[shard_step]), "ctx", -shard_step)
        summed = add_pair(summed, arrived)
    summed = lax.psum_scatter(summed, "section", scatter_dimension=1, tiled=True)
    query_out = (
        grad_query.reshape(groups, head_ratio, tok_rows, DH)
        .transpose(2, 0, 1, 3)
        .reshape(1, tok_rows, heads * DH)
    )
    return (query_out.astype(jnp.bfloat16), summed[0], summed[1])


def solution(mesh):
    placed = (
        P("section", "ctx", None),
        P("ctx", None),
        P("ctx", None),
        P("section", "ctx", None),
        P("ctx"),
    )
    return jax.shard_map(
        on_device,
        mesh=mesh,
        in_specs=placed,
        out_specs=(P("section", "ctx", None), P("ctx", "section"), P("ctx", "section")),
        check_vma=False,
    )
```

profile of v0, /device:TPU:6, one launch (start us, length us, event | category | flops | bytes accessed | tf_op | source)
XLA Modules:
  0.0 104.3 jit_solution(11517757769517617185)
XLA Ops:
  7.2 3.4 %collective-permute-start = (s32[128]{0:T(128)}, s32[128]{0:T(128)S(1)}, u32[]{:S(2)}, u32[]{:S(2)}) collective-permute-start(s32[128]{0:T(128)} %param.9), channel_id=1, source_target_pairs={{0,1},{1,2},{2,3},{3,4},{4,5},{5,6},{6,7},{7,8},{8,9},{9,10},{10,1... | collective-permute-start | bytes 1544 | tf_op jit(solution)/shard_map/ppermute | solution.py:13
  10.6 1.0 copy.48
  11.6 3.4 %collective-permute-start.1 = (bf16[128,512]{0,1:T(8,128)(2,1)S(1)}, bf16[128,512]{0,1:T(8,128)(2,1)}, u32[]{:S(2)}, u32[]{:S(2)}) collective-permute-start(bf16[128,512]{0,1:T(8,128)(2,1)S(1)} %copy.48), channel_id=1, source_target_pairs={{0,1},{1,2},{2,3},{3,4},{4,5},{5,6},{6,7},{7,8},{8,9},{9,10},{10,1... | collective-permute-start | bytes 393224 | tf_op jit(solution)/shard_map/ppermute | solution.py:13
  15.1 3.4 %collective-permute-start.4 = (bf16[128,512]{1,0:T(8,128)(2,1)}, bf16[128,512]{1,0:T(8,128)(2,1)}, u32[]{:S(2)}, u32[]{:S(2)}) collective-permute-start(bf16[128,512]{1,0:T(8,128)(2,1)} %param.7), channel_id=1, source_target_pairs={{0,1},{1,2},{2,3},{3,4},{4,5},{5,6},{6,7},{7,8},{8,9},{9,10},{10,1... | collective-permute-start | bytes 393224 | tf_op jit(solution)/shard_map/ppermute | solution.py:13
  18.5 0.7 broadcast_bitcast_fusion
  19.2 1.7 %copy.113 = bf16[128,512]{0,1:T(8,128)(2,1)} copy(bf16[128,512]{1,0:T(8,128)(2,1)} %param.7) | data formatting | bytes 262144 | tf_op jit(solution)/shard_map/reshape | solution.py:57
  20.9 3.5 %collective-permute-start.2 = (s32[128]{0:T(128)S(1)}, s32[128]{0:T(128)S(1)}, u32[]{:S(2)}, u32[]{:S(2)}) collective-permute-start(s32[128]{0:T(128)S(1)} %collective-permute-done), channel_id=1, source_target_pairs={{0,1},{1,2},{2,3},{3,4},{4,5},{5,6},{6,7},{7,8},{8,9},{9,10},{10,1... | collective-permute-start | bytes 1544 | tf_op jit(solution)/shard_map/ppermute | solution.py:13
  24.4 1.4 %copy.45 = bf16[1,128,2560]{1,2,0:T(8,128)(2,1)S(1)} copy(bf16[1,128,2560]{2,1,0:T(8,128)(2,1)} %param.5) | data formatting | bytes 1310720 | tf_op args[0]
  26.9 1.1 %copy.55 = bf16[4,640,128]{1,2,0:T(8,128)(2,1)} copy(bf16[4,640,128]{2,1,0:T(8,128)(2,1)S(1)} %bitcast.108) | data formatting | bytes 1310720 | tf_op jit(solution)/shard_map/reshape | solution.py:30
  28.3 0.4 select_reduce_fusion.5
  28.7 1.7 %copy.49 = bf16[128,4,128]{2,0,1:T(8,128)(2,1)} copy(bf16[128,4,128]{0,2,1:T(8,128)(2,1)} %bitcast.6) | data formatting | bytes 262144 | tf_op jit(solution)/shard_map/reshape | solution.py:56
  30.3 3.6 %collective-permute-start.3 = (bf16[128,512]{0,1:T(8,128)(2,1)}, bf16[128,512]{0,1:T(8,128)(2,1)}, u32[]{:S(2)}, u32[]{:S(2)}) collective-permute-start(bf16[128,512]{0,1:T(8,128)(2,1)} %collective-permute-done.1), channel_id=1, source_target_pairs={{0,1},{1,2},{2,3},{3,4},{4,5},{5,6},{6,7},{7,8},{8,9},{9,10},{10,1... | collective-permute-start | bytes 393224 | tf_op jit(solution)/shard_map/ppermute | solution.py:13
  34.0 1.3 %select_reduce_fusion.4 = (f32[4,640]{1,0:T(4,128)S(1)}, f32[4,640,128]{1,2,0:T(8,128)S(1)}) fusion(pred[640,128]{0,1:T(8,128)(4,1)S(1)} %get-tuple-element.10, bf16[4,640,128]{2,1,0:T(8,128)(2,1)S(1)} %bitcast.103, bf16[128,4,128]{2,0,1:T(8,128)(2,1)} %copy.49), kind=kOutput, calls=%fused_computation.28 | convolution fusion | flops 84866560 | bytes 2189312 | tf_op jit(solution)/shard_map/grd,gkd->grk/dot_general | solution.py:75
  35.3 1.7 %copy.57 = bf16[128,512]{0,1:T(8,128)(2,1)} copy(bf16[128,512]{1,0:T(8,128)(2,1)} %collective-permute-done.4) | data formatting | bytes 262144 | tf_op jit(solution)/shard_map/ppermute | solution.py:13
  37.0 3.1 %collective-permute-start.5 = (bf16[128,512]{1,0:T(8,128)(2,1)}, bf16[128,512]{1,0:T(8,128)(2,1)}, u32[]{:S(2)}, u32[]{:S(2)}) collective-permute-start(bf16[128,512]{1,0:T(8,128)(2,1)} %collective-permute-done.4), channel_id=1, source_target_pairs={{0,1},{1,2},{2,3},{3,4},{4,5},{5,6},{6,7},{7,8},{8,9},{9,10},{10,1... | collective-permute-start | bytes 393224 | tf_op jit(solution)/shard_map/ppermute | solution.py:13
  40.2 1.7 %copy.50 = bf16[128,4,128]{2,0,1:T(8,128)(2,1)} copy(bf16[128,4,128]{0,2,1:T(8,128)(2,1)} %bitcast.8) | data formatting | bytes 262144 | tf_op jit(solution)/shard_map/reshape | solution.py:56
  41.8 1.3 %select_reduce_fusion.3 = (f32[4,640]{1,0:T(4,128)S(1)}, f32[4,640,128]{1,2,0:T(8,128)S(1)}) fusion(pred[640,128]{0,1:T(8,128)(4,1)S(1)} %get-tuple-element.11, bf16[4,640,128]{2,1,0:T(8,128)(2,1)S(1)} %bitcast.104, bf16[128,4,128]{2,0,1:T(8,128)(2,1)} %copy.50), kind=kOutput, calls=%fused_computation.27 | convolution fusion | flops 84866560 | bytes 2189312 | tf_op jit(solution)/shard_map/grd,gkd->grk/dot_general | solution.py:75
  43.4 0.5 select_reduce_fusion
  44.0 0.7 copy-done.3
  44.7 1.2 %convolution_convert_fusion.1 = bf16[4,128,128]{1,2,0:T(8,128)(2,1)} fusion(bf16[4,640,128]{2,1,0:T(8,128)(2,1)S(1)} %bitcast.109, f32[4,640,128]{1,2,0:T(8,128)S(1)} %get-tuple-element.15, f32[4,640]{1,0:T(4,128)S(1)} %log_add_fusion, pred[640,128]{0,1:T(8,128)(4,1)S(1)} %get-tuple-element.10), kind=kOutput, calls=%fused_computation.32 | convolution fusion | flops 84934656 | bytes 2189312 | tf_op jit(solution)/shard_map/grk,grd->gkd/dot_general | solution.py:118
  45.8 1.2 %fusion.26 = f32[4,128,128]{1,2,0:T(8,128)} fusion(bf16[4,640,128]{2,1,0:T(8,128)(2,1)S(1)} %bitcast.110, f32[4,640,128]{1,2,0:T(8,128)S(1)} %get-tuple-element.17, f32[4,640]{1,0:T(4,128)S(1)} %log_add_fusion, pred[640,128]{0,1:T(8,128)(4,1)S(1)} %get-tuple-element.9), kind=kOutput, calls=%fused_computation.51 | convolution fusion | flops 84869120 | bytes 2320384 | tf_op jit(solution)/shard_map/grk,grd->gkd/dot_general | solution.py:118
  47.4 0.5 copy-done.14
  47.9 1.4 %convolution_add_fusion.1 = f32[4,640,128]{1,2,0:T(8,128)} fusion(f32[4,640,128]{1,2,0:T(8,128)S(1)} %fusion.28, bf16[4,128,128]{1,2,0:T(8,128)(2,1)S(1)} %bitcast.123, f32[4,640,128]{1,2,0:T(8,128)S(1)} %get-tuple-element.15, f32[4,640]{1,0:T(4,128)S(1)} %log_add_fusion, pred[640,128]{0,1:T(8,128)(4,1)S(1)} %get-tuple-element.10), kind=kOutput, calls=%fused_computation.1 | convolution fusion | flops 85196800 | bytes 4155392 | tf_op jit(solution)/shard_map/grk,gkd->grd/dot_general | solution.py:95
  49.4 1.2 %convolution_convert_fusion = bf16[4,128,128]{1,2,0:T(8,128)(2,1)} fusion(bf16[4,640,128]{2,1,0:T(8,128)(2,1)S(1)} %bitcast.111, f32[4,640,128]{1,2,0:T(8,128)S(1)} %get-tuple-element.13, f32[4,640]{1,0:T(4,128)S(1)} %log_add_fusion, pred[640,128]{0,1:T(8,128)(4,1)S(1)} %get-tuple-element.11), kind=kOutput, calls=%fused_computation.31 | convolution fusion | flops 84934656 | bytes 2189312 | tf_op jit(solution)/shard_map/grk,grd->gkd/dot_general | solution.py:118
  50.5 1.7 %copy.59 = bf16[128,512]{0,1:T(8,128)(2,1)} copy(bf16[128,512]{1,0:T(8,128)(2,1)} %collective-permute-done.5) | data formatting | bytes 262144 | tf_op jit(solution)/shard_map/ppermute | solution.py:13
  52.2 2.4 %fusion.11 = f32[4,640]{1,0:T(4,128)S(1)} fusion(f32[4,640,128]{1,2,0:T(8,128)} %convolution_add_fusion.1, bf16[4,128,128]{1,2,0:T(8,128)(2,1)} %bitcast.127, bf16[4,640,128]{1,2,0:T(8,128)(2,1)} %copy.55, f32[4,640,128]{1,2,0:T(8,128)} %copy-done, f32[4,640]{1,0:T(4,128)S(1)} %log_add_fusion, pred[640,128]{0,1:T(8,128)(4,1)S(1)} %get-tuple-element.11), kind=kOutput, calls=%fused_computation.30 | convolution fusion | flops 86177280 | bytes 3510272 | tf_op jit(solution)/shard_map/grk,gkd->grd/dot_general | solution.py:95
  54.7 1.4 %fusion.8 = bf16[4,640,128]{1,2,0:T(8,128)(2,1)} fusion(bf16[4,640,128]{2,1,0:T(8,128)(2,1)S(1)} %bitcast.112, bf16[4,128,128]{1,2,0:T(8,128)(2,1)S(1)} %bitcast.124, f32[4,640,128]{1,2,0:T(8,128)S(1)} %get-tuple-element.15, f32[4,640]{1,0:T(4,128)S(1)} %fusion.11, f32[4,640]{1,0:T(4,128)S(1)} %log_add_fusion, pred[640,128]{0,1:T(8,128)(4,1)S(1)} %get-tuple-element.10), kind=kOutput, calls=%fused_computation.18 | convolution fusion | flops 85852160 | bytes 2854912 | tf_op jit(solution)/shard_map/grd,gkd->grk/dot_general | solution.py:108
  56.1 1.4 %fusion.7 = bf16[4,640,128]{1,2,0:T(8,128)(2,1)} fusion(bf16[4,640,128]{2,1,0:T(8,128)(2,1)S(1)} %bitcast.113, bf16[4,128,128]{1,2,0:T(8,128)(2,1)S(1)} %bitcast.128, f32[4,640,128]{1,2,0:T(8,128)S(1)} %copy-done.1, f32[4,640]{1,0:T(4,128)S(1)} %fusion.11, f32[4,640]{1,0:T(4,128)S(1)} %log_add_fusion, pred[640,128]{0,1:T(8,128)(4,1)S(1)} %get-tuple-element.11), kind=kOutput, calls=%fused_computation.17 | convolution fusion | flops 85852160 | bytes 2854912 | tf_op jit(solution)/shard_map/grd,gkd->grk/dot_general | solution.py:108
  57.5 0.6 fusion.9
  58.5 1.1 %copy.87 = bf16[128,512]{1,0:T(8,128)(2,1)S(1)} copy(bf16[128,512]{0,1:T(8,128)(2,1)} %bitcast.130) | data formatting | bytes 262144 | tf_op jit(solution)/shard_map/convert_element_type | solution.py:19
  59.6 2.4 %collective-permute-start.9 = (bf16[128,512]{1,0:T(8,128)(2,1)S(1)}, bf16[128,512]{1,0:T(8,128)(2,1)S(1)}, u32[]{:S(2)}, u32[]{:S(2)}) collective-permute-start(bf16[128,512]{1,0:T(8,128)(2,1)S(1)} %copy.87), channel_id=1, source_target_pairs={{2,0},{3,1},{4,2},{5,3},{6,4},{7,5},{8,6},{9,7},{10,8},{11,9},{12,... | collective-permute-start | bytes 393224 | tf_op jit(solution)/shard_map/ppermute | solution.py:13
  62.0 3.1 %collective-permute-start.8 = (bf16[128,512]{1,0:T(8,128)(2,1)S(1)}, bf16[128,512]{1,0:T(8,128)(2,1)S(1)}, u32[]{:S(2)}, u32[]{:S(2)}) collective-permute-start(bf16[128,512]{1,0:T(8,128)(2,1)S(1)} %copy.83), channel_id=1, source_target_pairs={{1,0},{2,1},{3,2},{4,3},{5,4},{6,5},{7,6},{8,7},{9,8},{10,9},{11,1... | collective-permute-start | bytes 393224 | tf_op jit(solution)/shard_map/ppermute | solution.py:13
  65.1 1.1 %copy.84 = f32[128,512]{1,0:T(8,128)S(1)} copy(f32[128,512]{0,1:T(8,128)} %bitcast.120) | data formatting | bytes 524288 | tf_op jit(solution)/shard_map/reshape | solution.py:122
  66.2 1.5 %convolution_convert_fusion.2 = bf16[4,128,128]{1,2,0:T(8,128)(2,1)S(1)} fusion(bf16[4,640,128]{1,2,0:T(8,128)(2,1)} %fusion.7, bf16[4,640,128]{2,1,0:T(8,128)(2,1)S(1)} %bitcast.105), kind=kOutput, calls=%fused_computation.33 | convolution fusion | flops 83951616 | bytes 1441792 | tf_op jit(solution)/shard_map/grk,grd->gkd/dot_general | solution.py:115
  67.9 0.4 convolution_convert_fusion.3
  68.3 0.8 copy.74
  69.0 1.9 %collective-permute-start.6 = (bf16[128,512]{1,0:T(8,128)(2,1)}, bf16[128,512]{1,0:T(8,128)(2,1)}, u32[]{:S(2)}, u32[]{:S(2)}) collective-permute-start(bf16[128,512]{1,0:T(8,128)(2,1)} %copy.74), channel_id=1, source_target_pairs={{1,0},{2,1},{3,2},{4,3},{5,4},{6,5},{7,6},{8,7},{9,8},{10,9},{11,1... | collective-permute-start | bytes 393224 | tf_op jit(solution)/shard_map/ppermute | solution.py:13
  70.9 1.9 %collective-permute-start.7 = (bf16[128,512]{1,0:T(8,128)(2,1)S(1)}, bf16[128,512]{1,0:T(8,128)(2,1)}, u32[]{:S(2)}, u32[]{:S(2)}) collective-permute-start(bf16[128,512]{1,0:T(8,128)(2,1)S(1)} %copy.78), channel_id=1, source_target_pairs={{2,0},{3,1},{4,2},{5,3},{6,4},{7,5},{8,6},{9,7},{10,8},{11,9},{12,... | collective-permute-start | bytes 393224 | tf_op jit(solution)/shard_map/ppermute | solution.py:13
  72.9 0.8 convert_add_fusion
  74.1 1.1 %fusion.39 = f32[4,128,128]{1,2,0:T(8,128)} fusion(bf16[4,640,128]{1,2,0:T(8,128)(2,1)S(1)} %fusion.9, bf16[4,640,128]{2,1,0:T(8,128)(2,1)S(1)} %bitcast.107), kind=kOutput, calls=%fused_computation.68 | convolution fusion | flops 83886080 | bytes 1572864 | tf_op jit(solution)/shard_map/grk,grd->gkd/dot_general | solution.py:115
  75.2 1.1 %copy.75 = f32[128,512]{1,0:T(8,128)S(1)} copy(f32[128,512]{0,1:T(8,128)} %bitcast.119) | data formatting | bytes 524288 | tf_op jit(solution)/shard_map/reshape | solution.py:121
  76.3 2.0 %collective-permute-done.6 = bf16[128,512]{1,0:T(8,128)(2,1)} collective-permute-done((bf16[128,512]{1,0:T(8,128)(2,1)}, bf16[128,512]{1,0:T(8,128)(2,1)}, u32[]{:S(2)}, u32[]{:S(2)}) %collective-permute-start.6) | collective-permute-done | bytes 131104 | tf_op jit(solution)/shard_map/ppermute | solution.py:13
  78.3 1.1 %collective-permute-done.7 = bf16[128,512]{1,0:T(8,128)(2,1)} collective-permute-done((bf16[128,512]{1,0:T(8,128)(2,1)S(1)}, bf16[128,512]{1,0:T(8,128)(2,1)}, u32[]{:S(2)}, u32[]{:S(2)}) %collective-permute-start.7) | collective-permute-done | bytes 131104 | tf_op jit(solution)/shard_map/ppermute | solution.py:13
  79.4 1.7 %convert_add_fusion.1 = f32[128,512]{1,0:T(8,128)} fusion(bf16[128,512]{1,0:T(8,128)(2,1)} %collective-permute-done.7, f32[128,512]{1,0:T(8,128)S(1)} %copy.75, bf16[128,512]{1,0:T(8,128)(2,1)} %collective-permute-done.6), kind=kLoop, calls=%fused_computation.42 | loop fusion | flops 262144 | bytes 786432 | tf_op jit(solution)/shard_map/add | solution.py:35
  81.6 0.7 copy-done.6
  83.0 1.1 %copy.88 = bf16[1,128,2560]{2,1,0:T(8,128)(2,1)} copy(bf16[1,128,2560]{1,2,0:T(8,128)(2,1)S(1)} %bitcast.115) | data formatting | bytes 1310720
  84.1 1.7 %reduce-scatter.5.cloned.1.call-done = f32[128,256]{1,0:T(8,128)} async-done(((f32[128,512]{1,0:T(8,128)}), f32[128,256]{1,0:T(8,128)}) %reduce-scatter.5.cloned.1.call-update) | async-done | bytes 131088 | tf_op jit(solution)/shard_map/reduce_scatter | solution.py:132
  85.7 11.7 %reduce-scatter.3.cloned.1.call-done = f32[128,256]{1,0:T(8,128)} async-done(((f32[128,512]{1,0:T(8,128)}), f32[128,256]{1,0:T(8,128)}) %reduce-scatter.3.cloned.1.call-update) | async-done | bytes 131088 | tf_op jit(solution)/shard_map/reduce_scatter | solution.py:132
  (65 shorter events, 4.2 us)
Async XLA Ops:
  7.2 78.6 %reduce-scatter.5.cloned.1.call-start = ((), (), s32[]{:S(2)}) async-start(), calls=%async_computation.3 | async-start | bytes 393216 | tf_op jit(solution)/shard_map/reduce_scatter | solution.py:132
  7.2 13.7 %collective-permute-start = (s32[128]{0:T(128)}, s32[128]{0:T(128)S(1)}, u32[]{:S(2)}, u32[]{:S(2)}) collective-permute-start(s32[128]{0:T(128)} %param.9), channel_id=1, source_target_pairs={{0,1},{1,2},{2,3},{3,4},{4,5},{5,6},{6,7},{7,8},{8,9},{9,10},{10,1... | collective-permute-start | bytes 1544 | tf_op jit(solution)/shard_map/ppermute | solution.py:13
  11.6 17.0 %collective-permute-start.1 = (bf16[128,512]{0,1:T(8,128)(2,1)S(1)}, bf16[128,512]{0,1:T(8,128)(2,1)}, u32[]{:S(2)}, u32[]{:S(2)}) collective-permute-start(bf16[128,512]{0,1:T(8,128)(2,1)S(1)} %copy.48), channel_id=1, source_target_pairs={{0,1},{1,2},{2,3},{3,4},{4,5},{5,6},{6,7},{7,8},{8,9},{9,10},{10,1... | collective-permute-start | bytes 393224 | tf_op jit(solution)/shard_map/ppermute | solution.py:13
  15.1 20.3 %collective-permute-start.4 = (bf16[128,512]{1,0:T(8,128)(2,1)}, bf16[128,512]{1,0:T(8,128)(2,1)}, u32[]{:S(2)}, u32[]{:S(2)}) collective-permute-start(bf16[128,512]{1,0:T(8,128)(2,1)} %param.7), channel_id=1, source_target_pairs={{0,1},{1,2},{2,3},{3,4},{4,5},{5,6},{6,7},{7,8},{8,9},{9,10},{10,1... | collective-permute-start | bytes 393224 | tf_op jit(solution)/shard_map/ppermute | solution.py:13
  20.9 5.3 %copy-start.11 = (bf16[1,128,2560]{2,1,0:T(8,128)(2,1)S(1)}, bf16[1,128,2560]{2,1,0:T(8,128)(2,1)}, u32[]{:S(2)}) copy-start(bf16[1,128,2560]{2,1,0:T(8,128)(2,1)} %param.8) | copy-start | bytes 1966084
  20.9 7.1 %collective-permute-start.2 = (s32[128]{0:T(128)S(1)}, s32[128]{0:T(128)S(1)}, u32[]{:S(2)}, u32[]{:S(2)}) collective-permute-start(s32[128]{0:T(128)S(1)} %collective-permute-done), channel_id=1, source_target_pairs={{0,1},{1,2},{2,3},{3,4},{4,5},{5,6},{6,7},{7,8},{8,9},{9,10},{10,1... | collective-permute-start | bytes 1544 | tf_op jit(solution)/shard_map/ppermute | solution.py:13
  26.5 1.5 %copy-start.18 = (s32[128]{0:T(128)S(1)}, s32[128]{0:T(128)}, u32[]{:S(2)}) copy-start(s32[128]{0:T(128)} %param.9) | copy-start | bytes 1540
  26.5 1.7 %copy-start.7 = (bf16[128,512]{1,0:T(8,128)(2,1)S(1)}, bf16[128,512]{1,0:T(8,128)(2,1)}, u32[]{:S(2)}) copy-start(bf16[128,512]{1,0:T(8,128)(2,1)} %param.6) | copy-start | bytes 393220
  26.8 1.4 %copy-start.2 = (bf16[4,5,128,128]{3,2,1,0:T(8,128)(2,1)}, bf16[4,5,128,128]{3,2,1,0:T(8,128)(2,1)S(1)}, u32[]{:S(2)}) copy-start(bf16[4,5,128,128]{3,2,1,0:T(8,128)(2,1)S(1)} %copy.52) | copy-start | bytes 1966084
  30.3 9.8 %collective-permute-start.3 = (bf16[128,512]{0,1:T(8,128)(2,1)}, bf16[128,512]{0,1:T(8,128)(2,1)}, u32[]{:S(2)}, u32[]{:S(2)}) collective-permute-start(bf16[128,512]{0,1:T(8,128)(2,1)} %collective-permute-done.1), channel_id=1, source_target_pairs={{0,1},{1,2},{2,3},{3,4},{4,5},{5,6},{6,7},{7,8},{8,9},{9,10},{10,1... | collective-permute-start | bytes 393224 | tf_op jit(solution)/shard_map/ppermute | solution.py:13
  37.0 13.5 %collective-permute-start.5 = (bf16[128,512]{1,0:T(8,128)(2,1)}, bf16[128,512]{1,0:T(8,128)(2,1)}, u32[]{:S(2)}, u32[]{:S(2)}) collective-permute-start(bf16[128,512]{1,0:T(8,128)(2,1)} %collective-permute-done.4), channel_id=1, source_target_pairs={{0,1},{1,2},{2,3},{3,4},{4,5},{5,6},{6,7},{7,8},{8,9},{9,10},{10,1... | collective-permute-start | bytes 393224 | tf_op jit(solution)/shard_map/ppermute | solution.py:13
  43.1 6.2 %copy-start = (f32[4,640,128]{1,2,0:T(8,128)}, f32[4,640,128]{1,2,0:T(8,128)S(1)}, u32[]{:S(2)}) copy-start(f32[4,640,128]{1,2,0:T(8,128)S(1)} %get-tuple-element.13) | copy-start | bytes 3932164
  43.4 1.3 %copy-start.3 = (bf16[4,5,128,128]{3,2,1,0:T(8,128)(2,1)S(1)}, bf16[4,5,128,128]{3,2,1,0:T(8,128)(2,1)}, u32[]{:S(2)}) copy-start(bf16[4,5,128,128]{3,2,1,0:T(8,128)(2,1)} %copy-done.2) | copy-start | bytes 1966084
  45.8 1.2 %copy-start.12 = (bf16[128,512]{0,1:T(8,128)(2,1)S(1)}, bf16[128,512]{0,1:T(8,128)(2,1)}, u32[]{:S(2)}) copy-start(bf16[128,512]{0,1:T(8,128)(2,1)} %copy.113) | copy-start | bytes 393220
  47.0 0.9 copy-start.14
  52.2 2.4 %copy-start.4 = (bf16[4,5,128,128]{3,2,1,0:T(8,128)(2,1)S(1)}, bf16[4,5,128,128]{3,2,1,0:T(8,128)(2,1)}, u32[]{:S(2)}) copy-start(bf16[4,5,128,128]{3,2,1,0:T(8,128)(2,1)} %copy-done.2) | copy-start | bytes 1966084
  52.2 2.4 %copy-start.15 = (bf16[128,512]{0,1:T(8,128)(2,1)S(1)}, bf16[128,512]{0,1:T(8,128)(2,1)}, u32[]{:S(2)}) copy-start(bf16[128,512]{0,1:T(8,128)(2,1)} %copy.57) | copy-start | bytes 393220
  54.7 1.4 %copy-start.1 = (f32[4,640,128]{1,2,0:T(8,128)S(1)}, f32[4,640,128]{1,2,0:T(8,128)}, u32[]{:S(2)}) copy-start(f32[4,640,128]{1,2,0:T(8,128)} %copy-done) | copy-start | bytes 3932164
  54.7 1.4 %copy-start.16 = (bf16[128,512]{0,1:T(8,128)(2,1)S(1)}, bf16[128,512]{0,1:T(8,128)(2,1)}, u32[]{:S(2)}) copy-start(bf16[128,512]{0,1:T(8,128)(2,1)} %copy.59) | copy-start | bytes 393220
  56.1 1.4 %copy-start.13 = (bf16[128,512]{0,1:T(8,128)(2,1)S(1)}, bf16[128,512]{0,1:T(8,128)(2,1)}, u32[]{:S(2)}) copy-start(bf16[128,512]{0,1:T(8,128)(2,1)} %copy.113) | copy-start | bytes 393220
  57.5 0.9 copy-start.17
  58.5 9.3 %copy-start.5 = (bf16[4,640,128]{1,2,0:T(8,128)(2,1)S(1)}, bf16[4,640,128]{1,2,0:T(8,128)(2,1)}, u32[]{:S(2)}) copy-start(bf16[4,640,128]{1,2,0:T(8,128)(2,1)} %fusion.8) | copy-start | bytes 1966084
  59.6 13.3 %collective-permute-start.9 = (bf16[128,512]{1,0:T(8,128)(2,1)S(1)}, bf16[128,512]{1,0:T(8,128)(2,1)S(1)}, u32[]{:S(2)}, u32[]{:S(2)}) collective-permute-start(bf16[128,512]{1,0:T(8,128)(2,1)S(1)} %copy.87), channel_id=1, source_target_pairs={{2,0},{3,1},{4,2},{5,3},{6,4},{7,5},{8,6},{9,7},{10,8},{11,9},{12,... | collective-permute-start | bytes 393224 | tf_op jit(solution)/shard_map/ppermute | solution.py:13
  62.0 10.8 %collective-permute-start.8 = (bf16[128,512]{1,0:T(8,128)(2,1)S(1)}, bf16[128,512]{1,0:T(8,128)(2,1)S(1)}, u32[]{:S(2)}, u32[]{:S(2)}) collective-permute-start(bf16[128,512]{1,0:T(8,128)(2,1)S(1)} %copy.83), channel_id=1, source_target_pairs={{1,0},{2,1},{3,2},{4,3},{5,4},{6,5},{7,6},{8,7},{9,8},{10,9},{11,1... | collective-permute-start | bytes 393224 | tf_op jit(solution)/shard_map/ppermute | solution.py:13
  67.8 5.9 %copy-start.8 = (bf16[128,512]{1,0:T(8,128)(2,1)S(1)}, bf16[128,512]{1,0:T(8,128)(2,1)}, u32[]{:S(2)}) copy-start(bf16[128,512]{1,0:T(8,128)(2,1)} %param.6) | copy-start | bytes 393220
  69.0 9.3 %collective-permute-start.6 = (bf16[128,512]{1,0:T(8,128)(2,1)}, bf16[128,512]{1,0:T(8,128)(2,1)}, u32[]{:S(2)}, u32[]{:S(2)}) collective-permute-start(bf16[128,512]{1,0:T(8,128)(2,1)} %copy.74), channel_id=1, source_target_pairs={{1,0},{2,1},{3,2},{4,3},{5,4},{6,5},{7,6},{8,7},{9,8},{10,9},{11,1... | collective-permute-start | bytes 393224 | tf_op jit(solution)/shard_map/ppermute | solution.py:13
  70.9 8.5 %collective-permute-start.7 = (bf16[128,512]{1,0:T(8,128)(2,1)S(1)}, bf16[128,512]{1,0:T(8,128)(2,1)}, u32[]{:S(2)}, u32[]{:S(2)}) collective-permute-start(bf16[128,512]{1,0:T(8,128)(2,1)S(1)} %copy.78), channel_id=1, source_target_pairs={{2,0},{3,1},{4,2},{5,3},{6,4},{7,5},{8,6},{9,7},{10,8},{11,9},{12,... | collective-permute-start | bytes 393224 | tf_op jit(solution)/shard_map/ppermute | solution.py:13
  73.7 23.8 %reduce-scatter.3.cloned.1.call-start = ((), (), s32[]{:S(2)}) async-start(), calls=%async_computation.2 | async-start | bytes 393216 | tf_op jit(solution)/shard_map/reduce_scatter | solution.py:132
  74.1 7.0 %copy-start.9 = (bf16[128,4,128]{2,0,1:T(8,128)(2,1)S(1)}, bf16[128,4,128]{2,0,1:T(8,128)(2,1)}, u32[]{:S(2)}) copy-start(bf16[128,4,128]{2,0,1:T(8,128)(2,1)} %copy.49) | copy-start | bytes 393220
  81.1 1.1 %copy-start.6 = (bf16[4,640,128]{1,2,0:T(8,128)(2,1)S(1)}, bf16[4,640,128]{1,2,0:T(8,128)(2,1)}, u32[]{:S(2)}) copy-start(bf16[4,640,128]{1,2,0:T(8,128)(2,1)} %fusion.7) | copy-start | bytes 1966084
  81.1 1.1 %copy-start.10 = (bf16[128,4,128]{2,0,1:T(8,128)(2,1)S(1)}, bf16[128,4,128]{2,0,1:T(8,128)(2,1)}, u32[]{:S(2)}) copy-start(bf16[128,4,128]{2,0,1:T(8,128)(2,1)} %copy.50) | copy-start | bytes 393220
Sparse Core Ops, SparseCore 0:
  73.8 11.8 reduce-scatter.4
  88.6 8.8 reduce-scatter.2
where the time goes:
time: 106 us; the launch traced here: 104 us
  starting transfers between devices  29.9 us (28%)
  local copies, waits for them, and re-layouts  21.4 us (20%)
  matrix products  18.3 us (17%)
  waiting for transfers between devices  16.5 us (16%)
  between operations  14.5 us (14%)
  other arithmetic  3.57 us (3%)
    ppermute x10, starting transfers between devices, shifted(): return lax.ppermute(shard, axis, pairs)  29.8 us
    reduce_scatter x2, waiting for transfers between devices, on_device(): lax.psum_scatter(summed, 'section', scatter_dimension=1, tiled=True)  13.4 us
    unnamed x42, local copies, waits for them, and re-layouts  6.14 us
    dot_general x3, matrix products, output_part(): jnp.einsum('grk,gkd->grd', probs_low, value_rows, preferred_element_type=...  4.2 us
    dot_general x3, matrix products, backward_part(): jnp.einsum('grk,grd->gkd', probs_low, grad_rows, preferred_element_type=j...  3.51 us
    dot_general x3, matrix products, backward_part(): jnp.einsum('grd,gkd->grk', grad_rows, value_rows, preferred_element_type=...  3.39 us
    ppermute x2, local copies, waits for them, and re-layouts, shifted(): return lax.ppermute(shard, axis, pairs)  3.34 us
    reshape x2, local copies, waits for them, and re-layouts, on_device(): key_rows = key_block.reshape(tok_rows, groups, DH).transpose(1, 0, 2)  3.31 us
  transfers between devices with their start and end apart: 12, of which 4 were waited for; matrix products, arithmetic and copies ran while one was open for 31% of the time, Pallas kernels for 0%

commit v1 on v0

--- a/solution.py
+++ b/solution.py
@@ -1,10 +1,16 @@
+import functools
+
 import jax
 import jax.numpy as jnp
 from jax import lax
+from jax.experimental import pallas as pl
+from jax.experimental.pallas import tpu as pltpu
 from jax.sharding import PartitionSpec as P
 
 DH = 128
 DOC_SHARDS = 2
+LOG2E = 1.4426950408889634
+MESH = pl.DeviceIdType.MESH
 
 
 def shifted(shard, axis, by):
@@ -138,6 +144,339 @@
     return (query_out.astype(jnp.bfloat16), summed[0], summed[1])
 
 
+def dot(first, second, first_dim, second_dim):
+    return lax.dot_general(
+        first,
+        second,
+        (((first_dim,), (second_dim,)), ((), ())),
+        preferred_element_type=jnp.float32,
+    )
+
+
+def kernel(
+    cycle_size,
+    q_hbm,
+    k_hbm,
+    v_hbm,
+    g_hbm,
+    seg_hbm,
+    dq_hbm,
+    dk_ref,
+    dv_ref,
+    q_buf,
+    g_buf,
+    k_buf,
+    v_buf,
+    seg_buf,
+    bias,
+    s_buf,
+    gp_buf,
+    p_buf,
+    ds_buf,
+    dq_buf,
+    part,
+    got,
+    local_sem,
+    pair_send,
+    pair_recv,
+    near_send,
+    near_recv,
+    part_send,
+    part_recv,
+):
+    tok = k_hbm.shape[0]
+    half = q_buf.shape[2]
+    width = k_buf.shape[1]
+    groups = width // DH
+    ratio = half // width
+    rows = ratio * tok
+    shards = DOC_SHARDS + 1
+    scale = DH ** (-0.5)
+    me = lax.axis_index("ctx")
+    core = lax.axis_index("section")
+    other = 1 - core
+    my_cols = pl.ds(pl.multiple_of(core * half, DH), half)
+    other_cols = pl.ds(pl.multiple_of(other * half, DH), half)
+    my_heads = pl.ds(pl.multiple_of(core * width, DH), width)
+    steps = range(1, shards)
+
+    def block(step):
+        return slice((shards - 1 - step) * tok, (shards - step) * tok)
+
+    def block_ds(step):
+        return pl.ds((shards - 1 - step) * tok, tok)
+
+    barrier = pltpu.get_barrier_semaphore()
+    pl.semaphore_signal(barrier, inc=1, device_id={"section": other}, device_id_type=MESH)
+    greeted = 1
+    for step in steps:
+        has_next = me + step < cycle_size
+        has_prev = me >= step
+
+        @pl.when(has_next)
+        def _(step=step):
+            pl.semaphore_signal(barrier, inc=1, device_id={"ctx": me + step}, device_id_type=MESH)
+
+        @pl.when(has_prev)
+        def _(step=step):
+            pl.semaphore_signal(barrier, inc=1, device_id={"ctx": me - step}, device_id_type=MESH)
+
+        greeted = greeted + has_next.astype(jnp.int32) + has_prev.astype(jnp.int32)
+
+    local = [
+        pltpu.make_async_copy(source, target, local_sem.at[i])
+        for i, (source, target) in enumerate(
+            (
+                (k_hbm.at[:, my_heads], k_buf.at[block_ds(0), :]),
+                (q_hbm.at[0, :, my_cols], q_buf.at[0]),
+                (v_hbm.at[:, my_heads], v_buf.at[block_ds(0), :]),
+                (g_hbm.at[0, :, my_cols], g_buf.at[0]),
+                (seg_hbm, seg_buf.at[0]),
+            )
+        )
+    ]
+    for copy in local:
+        copy.start()
+    for step in steps:
+
+        @pl.when(me < step)
+        def _(step=step):
+            k_buf[block(step), :] = jnp.zeros((tok, width), jnp.bfloat16)
+            v_buf[block(step), :] = jnp.zeros((tok, width), jnp.bfloat16)
+            seg_buf[step] = jnp.full((1, tok), -1, jnp.int32)
+
+    pl.semaphore_wait(barrier, greeted)
+
+    def near_copies(step):
+        at = step - 1
+        pairs = (
+            (seg_hbm, seg_buf.at[step]),
+            (k_hbm.at[:, my_heads], k_buf.at[block_ds(step), :]),
+            (v_hbm.at[:, my_heads], v_buf.at[block_ds(step), :]),
+        )
+        return [
+            pltpu.make_async_remote_copy(
+                src_ref=source,
+                dst_ref=target,
+                send_sem=near_send.at[at, i],
+                recv_sem=near_recv.at[at, i],
+                device_id={"ctx": me + step},
+                device_id_type=MESH,
+            )
+            for i, (source, target) in enumerate(pairs)
+        ]
+
+    near = {step: near_copies(step) for step in steps}
+    for step in reversed(steps):
+
+        @pl.when(me + step < cycle_size)
+        def _(step=step):
+            for copy in near[step]:
+                copy.start()
+
+    def pair_copy(source, target, at):
+        return pltpu.make_async_remote_copy(
+            src_ref=source,
+            dst_ref=target,
+            send_sem=pair_send.at[at],
+            recv_sem=pair_recv.at[at],
+            device_id={"section": other},
+            device_id_type=MESH,
+        )
+
+    pair = [
+        pair_copy(q_hbm.at[0, :, other_cols], q_buf.at[1], 0),
+        pair_copy(g_hbm.at[0, :, other_cols], g_buf.at[1], 1),
+    ]
+    for copy in pair:
+        copy.start()
+
+    def head_cols(group, head):
+        start = (group * ratio + head) * DH
+        return slice(start, start + DH)
+
+    def stacked(buf, slot, group):
+        return jnp.concatenate([buf[slot, :, head_cols(group, h)] for h in range(ratio)], 0)
+
+    def products(step, slot):
+        for group in range(groups):
+            cols = slice(group * DH, (group + 1) * DH)
+            s_buf[group, slot, block(step), :] = dot(
+                k_buf[block(step), cols], stacked(q_buf, slot, group), 1, 1
+            )
+            gp_buf[group, slot, block(step), :] = dot(
+                v_buf[block(step), cols], stacked(g_buf, slot, group), 1, 1
+            )
+
+    def mask(step):
+        key_seg = jnp.broadcast_to(seg_buf[step].astype(jnp.float32), (tok, tok)).T
+        row_seg = seg_buf[0].astype(jnp.float32)
+        allowed = key_seg == row_seg
+        if step == 0:
+            key_at = lax.broadcasted_iota(jnp.int32, (tok, tok), 0)
+            row_at = lax.broadcasted_iota(jnp.int32, (tok, tok), 1)
+            allowed = allowed & (key_at <= row_at)
+        bias[block(step), :] = jnp.where(allowed, 0.0, -1e30)
+
+    for copy in local:
+        copy.wait()
+    mask(0)
+    products(0, 0)
+    for copy in pair:
+        copy.wait_recv()
+    products(0, 1)
+    for step in steps:
+
+        @pl.when(me >= step)
+        def _(step=step):
+            for copy in near[step]:
+                copy.wait_recv()
+
+        mask(step)
+        products(step, 0)
+        products(step, 1)
+
+    for group in range(groups):
+        for slot in range(2):
+            for head in range(ratio):
+                cols = slice(head * tok, (head + 1) * tok)
+                scores = s_buf[group, slot, :, cols] * (scale * LOG2E) + bias[...]
+                exps = jnp.exp2(scores - jnp.max(scores, 0, keepdims=True))
+                grad_probs = gp_buf[group, slot, :, cols]
+                inverse = 1.0 / jnp.sum(exps, 0, keepdims=True)
+                probs = exps * inverse
+                row_dot = jnp.sum(probs * grad_probs, 0, keepdims=True)
+                scaled = probs * (grad_probs - row_dot) * scale
+                at = slice(slot * rows + head * tok, slot * rows + (head + 1) * tok)
+                p_buf[group, :, at] = probs.astype(jnp.bfloat16)
+                ds_buf[group, :, at] = scaled.astype(jnp.bfloat16)
+
+    def all_rows(buf, group):
+        return jnp.concatenate([stacked(buf, 0, group), stacked(buf, 1, group)], 0)
+
+    def key_value_grads(step, group):
+        return (
+            dot(ds_buf[group, block(step), :], all_rows(q_buf, group), 1, 0),
+            dot(p_buf[group, block(step), :], all_rows(g_buf, group), 1, 0),
+        )
+
+    parts = {
+        step: pltpu.make_async_remote_copy(
+            src_ref=part.at[step - 1],
+            dst_ref=got.at[step - 1],
+            send_sem=part_send.at[step - 1],
+            recv_sem=part_recv.at[step - 1],
+            device_id={"ctx": me - step},
+            device_id_type=MESH,
+        )
+        for step in steps
+    }
+    for step in reversed(steps):
+        for group in range(groups):
+            cols = slice(group * DH, (group + 1) * DH)
+            grad_key, grad_value = key_value_grads(step, group)
+            part[step - 1, 0, :, cols] = grad_key.astype(jnp.bfloat16)
+            part[step - 1, 1, :, cols] = grad_value.astype(jnp.bfloat16)
+
+        @pl.when(me >= step)
+        def _(step=step):
+            parts[step].start()
+
+    def query_grads(slot):
+        for group in range(groups):
+            cols = slice(group * DH, (group + 1) * DH)
+            flipped = dot(
+                k_buf[:, cols], ds_buf[group, :, slot * rows : (slot + 1) * rows], 0, 0
+            )
+            for head in range(ratio):
+                dq_buf[slot, :, head_cols(group, head)] = flipped[
+                    :, head * tok : (head + 1) * tok
+                ].T.astype(jnp.bfloat16)
+
+    query_grads(1)
+    query_send = pair_copy(dq_buf.at[1], dq_hbm.at[0, :, my_cols], 2)
+    query_send.start()
+    query_grads(0)
+    query_keep = pltpu.make_async_copy(dq_buf.at[0], dq_hbm.at[0, :, my_cols], local_sem.at[0])
+    query_keep.start()
+    for group in range(groups):
+        cols = slice(group * DH, (group + 1) * DH)
+        grad_key, grad_value = key_value_grads(0, group)
+        dk_ref[:, cols] = grad_key
+        dv_ref[:, cols] = grad_value
+    for step in steps:
+
+        @pl.when(me + step < cycle_size)
+        def _(step=step):
+            parts[step].wait_recv()
+            dk_ref[...] += got[step - 1, 0].astype(jnp.float32)
+            dv_ref[...] += got[step - 1, 1].astype(jnp.float32)
+
+    query_keep.wait()
+    query_send.wait()
+    for copy in pair:
+        copy.wait_send()
+    for step in steps:
+
+        @pl.when(me + step < cycle_size)
+        def _(step=step):
+            for copy in near[step]:
+                copy.wait_send()
+
+        @pl.when(me >= step)
+        def _(step=step):
+            parts[step].wait_send()
+
+
+def by_heads(cycle_size, queries, keys, values, cotangent, segment_ids):
+    tok = keys.shape[0]
+    half = queries.shape[2] // 2
+    width = keys.shape[1] // 2
+    groups = width // DH
+    rows = half // groups
+    rows = rows // DH * tok
+    window = (DOC_SHARDS + 1) * tok
+    bf16, f32 = jnp.bfloat16, jnp.float32
+    anywhere = pl.BlockSpec(memory_space=pl.ANY)
+    in_vmem = pl.BlockSpec(memory_space=pltpu.VMEM)
+    dma = pltpu.SemaphoreType.DMA
+    return pl.pallas_call(
+        functools.partial(kernel, cycle_size),
+        out_shape=(
+            jax.ShapeDtypeStruct(queries.shape, bf16),
+            jax.ShapeDtypeStruct((tok, width), f32),
+            jax.ShapeDtypeStruct((tok, width), f32),
+        ),
+        in_specs=[anywhere] * 5,
+        out_specs=(anywhere, in_vmem, in_vmem),
+        scratch_shapes=[
+            pltpu.VMEM((2, tok, half), bf16),
+            pltpu.VMEM((2, tok, half), bf16),
+            pltpu.VMEM((window, width), bf16),
+            pltpu.VMEM((window, width), bf16),
+            pltpu.VMEM((DOC_SHARDS + 1, 1, tok), jnp.int32),
+            pltpu.VMEM((window, tok), f32),
+            pltpu.VMEM((groups, 2, window, rows), f32),
+            pltpu.VMEM((groups, 2, window, rows), f32),
+            pltpu.VMEM((groups, window, 2 * rows), bf16),
+            pltpu.VMEM((groups, window, 2 * rows), bf16),
+            pltpu.VMEM((2, tok, half), bf16),
+            pltpu.VMEM((DOC_SHARDS, 2, tok, width), bf16),
+            pltpu.VMEM((DOC_SHARDS, 2, tok, width), bf16),
+            dma((5,)),
+            dma((3,)),
+            dma((3,)),
+            dma((DOC_SHARDS, 3)),
+            dma((DOC_SHARDS, 3)),
+            dma((DOC_SHARDS,)),
+            dma((DOC_SHARDS,)),
+        ],
+        compiler_params=pltpu.CompilerParams(
+            collective_id=0, has_side_effects=True, vmem_limit_bytes=48 << 20
+        ),
+    )(queries, keys, values, cotangent, segment_ids.reshape(1, tok))
+
+
 def solution(mesh):
     placed = (
         P("section", "ctx", None),
@@ -146,8 +485,18 @@
         P("section", "ctx", None),
         P("ctx"),
     )
+    cycle_size = mesh.shape["ctx"]
+    pairs = mesh.shape["section"] == 2
+
+    def step(queries, keys, values, cotangent, segment_ids):
+        tok, width = keys.shape
+        halves = pairs and queries.shape[0] == 1 and tok % DH == 0 and width % (2 * DH) == 0
+        if halves:
+            return by_heads(cycle_size, queries, keys, values, cotangent, segment_ids)
+        return on_device(queries, keys, values, cotangent, segment_ids)
+
     return jax.shard_map(
-        on_device,
+        step,
         mesh=mesh,
         in_specs=placed,
         out_specs=(P("section", "ctx", None), P("ctx", "section"), P("ctx", "section")),

time: 106 us -> 28.4 us (0.27); the launches traced: 104 us -> 28.1 us
  starting transfers between devices: 29.9 us -> 0 us
  Pallas kernels: 0 us -> 20.7 us
  matrix products: 18.3 us -> 0 us
  waiting for transfers between devices: 16.5 us -> 0 us
  local copies, waits for them, and re-layouts: 21.4 us -> 6.78 us
  between operations: 14.5 us -> 0.65 us
  other arithmetic: 3.57 us -> 0 us
    ppermute x10 -> x0, starting transfers between devices: 29.8 us -> none  [shifted(): return lax.ppermute(shard, axis, pairs)]
    pallas_call x0 -> x1, Pallas kernels: none -> 20.7 us  [by_heads(): pl.pallas_call(functools.partial(kernel, cycle_size), out_shape=(jax.Shap...]
    dot_general x18 -> x0, matrix products: 18.3 us -> none  [the longest x3 4.2 us: output_part(): jnp.einsum('grk,gkd->grd', probs_low, value_rows, preferred_element_type=...]
    reduce_scatter x2 -> x0, waiting for transfers between devices: 13.4 us -> none  [on_device(): lax.psum_scatter(summed, 'section', scatter_dimension=1, tiled=True)]
    reshape x6 -> x0, local copies, waits for them, and re-layouts: 8.23 us -> none  [the longest x2 3.31 us: on_device(): key_rows = key_block.reshape(tok_rows, groups, DH).transpose(1, 0, 2)]
    ppermute x2 -> x0, local copies, waits for them, and re-layouts: 3.34 us -> none  [shifted(): return lax.ppermute(shard, axis, pairs)]
    ppermute x10 -> x0, waiting for transfers between devices: 3.1 us -> none  [shifted(): return lax.ppermute(shard, axis, pairs)]
    add x7 -> x0, other arithmetic: 2.51 us -> none  [the longest x2 2.46 us: add_pair(): return (first[0] + second[0], first[1] + second[1])]
  transfers between devices with their start and end apart: 12 -> 0, of which waited for: 4 -> 0; matrix products, arithmetic and copies ran while one was open for 31% -> 0% of each run, Pallas kernels for 0% -> 0%
where the time goes in v1:
time: 28.4 us; the launch traced here: 28.1 us
  Pallas kernels  20.7 us (73%)
  local copies, waits for them, and re-layouts  6.78 us (24%)
  between operations  0.65 us (2%)
    pallas_call x1, Pallas kernels, by_heads(): pl.pallas_call(functools.partial(kernel, cycle_size), out_shape=(jax.Shap...  20.7 us
    unnamed x13, local copies, waits for them, and re-layouts  6.78 us

profile of v1, /device:TPU:6, one launch (start us, length us, event | category | flops | bytes accessed | tf_op | source)
XLA Modules:
  0.0 28.1 jit_solution(10801333131763173829)
XLA Ops:
  0.6 0.0 copy-start.4
  0.6 0.6 %copy-done.4 = s32[128]{0:T(128)S(1)} copy-done((s32[128]{0:T(128)S(1)}, s32[128]{0:T(128)}, u32[]{:S(2)}) %copy-start.4) | copy-done | bytes 536
  1.3 0.0 copy-start
  1.3 1.1 %copy-done = bf16[1,128,2560]{2,1,0:T(8,128)(2,1)S(1)} copy-done((bf16[1,128,2560]{2,1,0:T(8,128)(2,1)S(1)}, bf16[1,128,2560]{2,1,0:T(8,128)(2,1)}, u32[]{:S(2)}) %copy-start) | copy-done | bytes 655384
  2.4 0.0 copy-start.1
  2.4 1.1 %copy-done.1 = bf16[1,128,2560]{2,1,0:T(8,128)(2,1)S(1)} copy-done((bf16[1,128,2560]{2,1,0:T(8,128)(2,1)S(1)}, bf16[1,128,2560]{2,1,0:T(8,128)(2,1)}, u32[]{:S(2)}) %copy-start.1) | copy-done | bytes 655384
  3.5 0.0 copy-start.2
  3.5 0.9 %copy-done.2 = bf16[128,512]{1,0:T(8,128)(2,1)S(1)} copy-done((bf16[128,512]{1,0:T(8,128)(2,1)S(1)}, bf16[128,512]{1,0:T(8,128)(2,1)}, u32[]{:S(2)}) %copy-start.2) | copy-done | bytes 131096
  4.4 0.0 copy-start.3
  4.4 0.9 %copy-done.3 = bf16[128,512]{1,0:T(8,128)(2,1)S(1)} copy-done((bf16[128,512]{1,0:T(8,128)(2,1)S(1)}, bf16[128,512]{1,0:T(8,128)(2,1)}, u32[]{:S(2)}) %copy-start.3) | copy-done | bytes 131096
  5.3 20.7 %shard_map.76 = (bf16[1,128,2560]{2,1,0:T(8,128)(2,1)S(1)}, f32[128,256]{1,0:T(8,128)S(1)}, f32[128,256]{1,0:T(8,128)S(1)}) custom-call(bf16[1,128,2560]{2,1,0:T(8,128)(2,1)S(1)} %copy-done, bf16[128,512]{1,0:T(8,128)(2,1)S(1)} %copy-done.2, bf16[128,512]{1,0:T(8,128)(2,1)S(1)} %copy-done.3, bf16[1,128,2560]{2,1,0:T(8,128)(2,1)S(1)} %copy-done.1, ...), custom_call_target="tpu_custom_call" | custom-call | tf_op jit(solution)/shard_map/pallas_call | solution.py:443
  26.0 0.8 %copy.11 = bf16[1,128,2560]{2,1,0:T(8,128)(2,1)} copy(bf16[1,128,2560]{2,1,0:T(8,128)(2,1)S(1)} %get-tuple-element.6) | data formatting | bytes 1310720
  26.8 0.7 %copy.12 = f32[128,256]{1,0:T(8,128)} copy(f32[128,256]{1,0:T(8,128)S(1)} %get-tuple-element.7) | data formatting | bytes 262144
  27.5 0.7 %copy.13 = f32[128,256]{1,0:T(8,128)} copy(f32[128,256]{1,0:T(8,128)S(1)} %get-tuple-element.8) | data formatting | bytes 262144
Async XLA Ops:
  0.6 0.7 %copy-start.4 = (s32[128]{0:T(128)S(1)}, s32[128]{0:T(128)}, u32[]{:S(2)}) copy-start(s32[128]{0:T(128)} %param.9) | copy-start | bytes 1540
  1.3 1.1 %copy-start = (bf16[1,128,2560]{2,1,0:T(8,128)(2,1)S(1)}, bf16[1,128,2560]{2,1,0:T(8,128)(2,1)}, u32[]{:S(2)}) copy-start(bf16[1,128,2560]{2,1,0:T(8,128)(2,1)} %q_hbm.1) | copy-start | bytes 1966084
  2.4 1.1 %copy-start.1 = (bf16[1,128,2560]{2,1,0:T(8,128)(2,1)S(1)}, bf16[1,128,2560]{2,1,0:T(8,128)(2,1)}, u32[]{:S(2)}) copy-start(bf16[1,128,2560]{2,1,0:T(8,128)(2,1)} %g_hbm.1) | copy-start | bytes 1966084
  3.5 0.9 %copy-start.2 = (bf16[128,512]{1,0:T(8,128)(2,1)S(1)}, bf16[128,512]{1,0:T(8,128)(2,1)}, u32[]{:S(2)}) copy-start(bf16[128,512]{1,0:T(8,128)(2,1)} %k_hbm.1) | copy-start | bytes 393220
  4.4 0.9 %copy-start.3 = (bf16[128,512]{1,0:T(8,128)(2,1)S(1)}, bf16[128,512]{1,0:T(8,128)(2,1)}, u32[]{:S(2)}) copy-start(bf16[128,512]{1,0:T(8,128)(2,1)} %v_hbm.1) | copy-start | bytes 393220

commit v2 on v0

--- a/solution.py
+++ b/solution.py
@@ -1,10 +1,18 @@
+import functools
+
 import jax
 import jax.numpy as jnp
 from jax import lax
+from jax.experimental import pallas as pl
+from jax.experimental.pallas import tpu as pltpu
 from jax.sharding import PartitionSpec as P
 
 DH = 128
 DOC_SHARDS = 2
+LOG2E = 1.4426950408889634
+MESH = pl.DeviceIdType.MESH
+VMEM_BYTES = 63 << 20
+PIECES = 4
 
 
 def shifted(shard, axis, by):
@@ -138,6 +146,396 @@
     return (query_out.astype(jnp.bfloat16), summed[0], summed[1])
 
 
+def dot(first, second, first_dim, second_dim):
+    return lax.dot_general(
+        first,
+        second,
+        (((first_dim,), (second_dim,)), ((), ())),
+        preferred_element_type=jnp.float32,
+    )
+
+
+def kernel(
+    cycle_size,
+    q_hbm,
+    k_hbm,
+    v_hbm,
+    g_hbm,
+    seg_hbm,
+    dq_hbm,
+    dk_ref,
+    dv_ref,
+    q_buf,
+    g_buf,
+    k_buf,
+    v_buf,
+    seg_buf,
+    bias,
+    s_buf,
+    gp_buf,
+    p_buf,
+    ds_buf,
+    dq_buf,
+    part,
+    got,
+    local_sem,
+    pair_send,
+    pair_recv,
+    seg_send,
+    seg_recv,
+    near_send,
+    near_recv,
+    part_send,
+    part_recv,
+):
+    tok = k_hbm.shape[0]
+    groups = k_buf.shape[0]
+    share = q_buf.shape[3]
+    ratio = share // DH
+    rows = ratio * tok
+    shards = DOC_SHARDS + 1
+    scale = DH ** (-0.5)
+    me = lax.axis_index("ctx")
+    core = lax.axis_index("section")
+    other = 1 - core
+    steps = range(1, shards)
+
+    def query_cols(owner, group):
+        return pl.ds(pl.multiple_of((owner * groups + group) * share, DH), share)
+
+    def key_cols(group):
+        return pl.ds(pl.multiple_of((core * groups + group) * DH, DH), DH)
+
+    def block(step):
+        return slice((shards - 1 - step) * tok, (shards - step) * tok)
+
+    def block_ds(step):
+        return pl.ds((shards - 1 - step) * tok, tok)
+
+    barrier = pltpu.get_barrier_semaphore()
+    pl.semaphore_signal(barrier, inc=1, device_id={"section": other}, device_id_type=MESH)
+    greeted = 1
+    for step in steps:
+        has_next = me + step < cycle_size
+        has_prev = me >= step
+
+        @pl.when(has_next)
+        def _(step=step):
+            pl.semaphore_signal(barrier, inc=1, device_id={"ctx": me + step}, device_id_type=MESH)
+
+        @pl.when(has_prev)
+        def _(step=step):
+            pl.semaphore_signal(barrier, inc=1, device_id={"ctx": me - step}, device_id_type=MESH)
+
+        greeted = greeted + has_next.astype(jnp.int32) + has_prev.astype(jnp.int32)
+
+    def own_copies(group):
+        pairs = (
+            (k_hbm.at[:, key_cols(group)], k_buf.at[group, block_ds(0), :]),
+            (q_hbm.at[0, :, query_cols(core, group)], q_buf.at[0, group]),
+            (v_hbm.at[:, key_cols(group)], v_buf.at[group, block_ds(0), :]),
+            (g_hbm.at[0, :, query_cols(core, group)], g_buf.at[0, group]),
+        )
+        return [
+            pltpu.make_async_copy(source, target, local_sem.at[group, i])
+            for i, (source, target) in enumerate(pairs)
+        ]
+
+    own = [own_copies(group) for group in range(groups)]
+    own_seg = pltpu.make_async_copy(seg_hbm, seg_buf.at[0], local_sem.at[groups, 0])
+    own_seg.start()
+    for copies in own:
+        for copy in copies:
+            copy.start()
+    for step in steps:
+
+        @pl.when(me < step)
+        def _(step=step):
+            for group in range(groups):
+                k_buf[group, block(step), :] = jnp.zeros((tok, DH), jnp.bfloat16)
+                v_buf[group, block(step), :] = jnp.zeros((tok, DH), jnp.bfloat16)
+            seg_buf[step] = jnp.full((1, tok), -1, jnp.int32)
+
+    pl.semaphore_wait(barrier, greeted)
+
+    def to_next(source, target, step, send, recv):
+        return pltpu.make_async_remote_copy(
+            src_ref=source,
+            dst_ref=target,
+            send_sem=send,
+            recv_sem=recv,
+            device_id={"ctx": me + step},
+            device_id_type=MESH,
+        )
+
+    def near_copies(step, group):
+        at = step - 1
+        pairs = (
+            (k_hbm.at[:, key_cols(group)], k_buf.at[group, block_ds(step), :]),
+            (v_hbm.at[:, key_cols(group)], v_buf.at[group, block_ds(step), :]),
+        )
+        return [
+            to_next(source, target, step, near_send.at[at, group, i], near_recv.at[at, group, i])
+            for i, (source, target) in enumerate(pairs)
+        ]
+
+    near = {step: [near_copies(step, group) for group in range(groups)] for step in steps}
+    near_seg = {
+        step: to_next(
+            seg_hbm, seg_buf.at[step], step, seg_send.at[step - 1], seg_recv.at[step - 1]
+        )
+        for step in steps
+    }
+
+    def pair_copy(source, target, group, at):
+        return pltpu.make_async_remote_copy(
+            src_ref=source,
+            dst_ref=target,
+            send_sem=pair_send.at[group, at],
+            recv_sem=pair_recv.at[group, at],
+            device_id={"section": other},
+            device_id_type=MESH,
+        )
+
+    pair = [
+        [
+            pair_copy(q_hbm.at[0, :, query_cols(other, group)], q_buf.at[1, group], group, 0),
+            pair_copy(g_hbm.at[0, :, query_cols(other, group)], g_buf.at[1, group], group, 1),
+        ]
+        for group in range(groups)
+    ]
+    for group in range(groups):
+        for step in reversed(steps):
+
+            @pl.when(me + step < cycle_size)
+            def _(step=step, group=group):
+                if group == 0:
+                    near_seg[step].start()
+                for copy in near[step][group]:
+                    copy.start()
+
+        for copy in pair[group]:
+            copy.start()
+
+    def head_cols(head):
+        return slice(head * DH, (head + 1) * DH)
+
+    def stacked(buf, slot, group):
+        return jnp.concatenate([buf[slot, group, :, head_cols(h)] for h in range(ratio)], 0)
+
+    def products(step, slot, group):
+        s_buf[group, slot, block(step), :] = dot(
+            k_buf[group, block(step), :], stacked(q_buf, slot, group), 1, 1
+        )
+        gp_buf[group, slot, block(step), :] = dot(
+            v_buf[group, block(step), :], stacked(g_buf, slot, group), 1, 1
+        )
+
+    def mask(step):
+        key_seg = jnp.broadcast_to(seg_buf[step].astype(jnp.float32), (tok, tok)).T
+        row_seg = seg_buf[0].astype(jnp.float32)
+        allowed = key_seg == row_seg
+        if step == 0:
+            key_at = lax.broadcasted_iota(jnp.int32, (tok, tok), 0)
+            row_at = lax.broadcasted_iota(jnp.int32, (tok, tok), 1)
+            allowed = allowed & (key_at <= row_at)
+        bias[block(step), :] = jnp.where(allowed, 0.0, -1e30)
+
+    def probabilities(group, slot):
+        for head in range(ratio):
+            cols = slice(head * tok, (head + 1) * tok)
+            scores = s_buf[group, slot, :, cols] * (scale * LOG2E) + bias[...]
+            exps = jnp.exp2(scores - jnp.max(scores, 0, keepdims=True))
+            grad_probs = gp_buf[group, slot, :, cols]
+            inverse = 1.0 / jnp.sum(exps, 0, keepdims=True)
+            probs = exps * inverse
+            row_dot = jnp.sum(probs * grad_probs, 0, keepdims=True)
+            scaled = probs * (grad_probs - row_dot) * scale
+            at = slice(slot * rows + head * tok, slot * rows + (head + 1) * tok)
+            p_buf[group, :, at] = probs.astype(jnp.bfloat16)
+            ds_buf[group, :, at] = scaled.astype(jnp.bfloat16)
+
+    def all_rows(buf, group):
+        return jnp.concatenate([stacked(buf, 0, group), stacked(buf, 1, group)], 0)
+
+    def key_value_grads(step, group):
+        return (
+            dot(ds_buf[group, block(step), :], all_rows(q_buf, group), 1, 0),
+            dot(p_buf[group, block(step), :], all_rows(g_buf, group), 1, 0),
+        )
+
+    def query_grads(group, slot):
+        flipped = dot(k_buf[group], ds_buf[group, :, slot * rows : (slot + 1) * rows], 0, 0)
+        for head in range(ratio):
+            dq_buf[slot, group, :, head_cols(head)] = flipped[
+                :, head * tok : (head + 1) * tok
+            ].T.astype(jnp.bfloat16)
+
+    def part_copy(step, group):
+        return pltpu.make_async_remote_copy(
+            src_ref=part.at[group, step - 1],
+            dst_ref=got.at[group, step - 1],
+            send_sem=part_send.at[group, step - 1],
+            recv_sem=part_recv.at[group, step - 1],
+            device_id={"ctx": me - step},
+            device_id_type=MESH,
+        )
+
+    parts = [{step: part_copy(step, group) for step in steps} for group in range(groups)]
+    query_send = [
+        pair_copy(dq_buf.at[1, group], dq_hbm.at[0, :, query_cols(core, group)], group, 2)
+        for group in range(groups)
+    ]
+    query_keep = [
+        pltpu.make_async_copy(
+            dq_buf.at[0, group], dq_hbm.at[0, :, query_cols(core, group)], local_sem.at[group, 4]
+        )
+        for group in range(groups)
+    ]
+
+    own_seg.wait()
+    mask(0)
+    for group in range(groups):
+        for copy in own[group]:
+            copy.wait()
+        products(0, 0, group)
+    for group in range(groups):
+        for copy in pair[group]:
+            copy.wait_recv()
+        products(0, 1, group)
+    for group in range(groups):
+        for step in steps:
+
+            @pl.when(me >= step)
+            def _(step=step, group=group):
+                if group == 0:
+                    near_seg[step].wait_recv()
+                for copy in near[step][group]:
+                    copy.wait_recv()
+
+            if group == 0:
+                mask(step)
+            products(step, 0, group)
+            products(step, 1, group)
+        probabilities(group, 0)
+        probabilities(group, 1)
+        for step in reversed(steps):
+            grad_key, grad_value = key_value_grads(step, group)
+            part[group, step - 1, 0] = grad_key.astype(jnp.bfloat16)
+            part[group, step - 1, 1] = grad_value.astype(jnp.bfloat16)
+
+            @pl.when(me >= step)
+            def _(step=step, group=group):
+                parts[group][step].start()
+
+        query_grads(group, 1)
+        query_send[group].start()
+        query_grads(group, 0)
+        query_keep[group].start()
+        grad_key, grad_value = key_value_grads(0, group)
+        dk_ref[:, head_cols(group)] = grad_key
+        dv_ref[:, head_cols(group)] = grad_value
+    for group in range(groups):
+        for step in steps:
+
+            @pl.when(me + step < cycle_size)
+            def _(step=step, group=group):
+                parts[group][step].wait_recv()
+                dk_ref[:, head_cols(group)] += got[group, step - 1, 0].astype(jnp.float32)
+                dv_ref[:, head_cols(group)] += got[group, step - 1, 1].astype(jnp.float32)
+
+    for group in range(groups):
+        query_keep[group].wait()
+        query_send[group].wait()
+        for copy in pair[group]:
+            copy.wait_send()
+        for step in steps:
+
+            @pl.when(me + step < cycle_size)
+            def _(step=step, group=group):
+                if group == 0:
+                    near_seg[step].wait_send()
+                for copy in near[step][group]:
+                    copy.wait_send()
+
+            @pl.when(me >= step)
+            def _(step=step, group=group):
+                parts[group][step].wait_send()
+
+
+def hand_over(dq_in, dk_in, dv_in, dq_out, dk_out, dv_out, sem):
+    piece = dq_in.shape[1] // PIECES
+    cuts = [pl.ds(i * piece, piece) for i in range(PIECES)]
+    pairs = [(dq_in.at[:, cut], dq_out.at[:, cut]) for cut in cuts]
+    pairs += [(dk_in, dk_out), (dv_in, dv_out)]
+    copies = [pltpu.make_async_copy(*pair, sem.at[i]) for i, pair in enumerate(pairs)]
+    for copy in copies:
+        copy.start()
+    for copy in copies:
+        copy.wait()
+
+
+def by_heads(cycle_size, queries, keys, values, cotangent, segment_ids):
+    tok = keys.shape[0]
+    half = queries.shape[2] // 2
+    width = keys.shape[1] // 2
+    groups = width // DH
+    rows = half // groups
+    rows = rows // DH * tok
+    window = (DOC_SHARDS + 1) * tok
+    bf16, f32 = jnp.bfloat16, jnp.float32
+    anywhere = pl.BlockSpec(memory_space=pl.ANY)
+    in_hbm = pl.BlockSpec(memory_space=pltpu.HBM)
+    in_vmem = pl.BlockSpec(memory_space=pltpu.VMEM)
+    dma = pltpu.SemaphoreType.DMA
+    shapes = (
+        jax.ShapeDtypeStruct(queries.shape, bf16),
+        jax.ShapeDtypeStruct((tok, width), f32),
+        jax.ShapeDtypeStruct((tok, width), f32),
+    )
+    grads = pl.pallas_call(
+        functools.partial(kernel, cycle_size),
+        out_shape=shapes,
+        in_specs=[in_hbm] * 5,
+        out_specs=(anywhere, in_vmem, in_vmem),
+        scratch_shapes=[
+            pltpu.VMEM((2, groups, tok, half // groups), bf16),
+            pltpu.VMEM((2, groups, tok, half // groups), bf16),
+            pltpu.VMEM((groups, window, DH), bf16),
+            pltpu.VMEM((groups, window, DH), bf16),
+            pltpu.VMEM((DOC_SHARDS + 1, 1, tok), jnp.int32),
+            pltpu.VMEM((window, tok), f32),
+            pltpu.VMEM((groups, 2, window, rows), f32),
+            pltpu.VMEM((groups, 2, window, rows), f32),
+            pltpu.VMEM((groups, window, 2 * rows), bf16),
+            pltpu.VMEM((groups, window, 2 * rows), bf16),
+            pltpu.VMEM((2, groups, tok, half // groups), bf16),
+            pltpu.VMEM((groups, DOC_SHARDS, 2, tok, DH), bf16),
+            pltpu.VMEM((groups, DOC_SHARDS, 2, tok, DH), bf16),
+            dma((groups + 1, 5)),
+            dma((groups, 3)),
+            dma((groups, 3)),
+            dma((DOC_SHARDS,)),
+            dma((DOC_SHARDS,)),
+            dma((DOC_SHARDS, groups, 2)),
+            dma((DOC_SHARDS, groups, 2)),
+            dma((groups, DOC_SHARDS)),
+            dma((groups, DOC_SHARDS)),
+        ],
+        compiler_params=pltpu.CompilerParams(
+            collective_id=0, has_side_effects=True, vmem_limit_bytes=VMEM_BYTES
+        ),
+    )(queries, keys, values, cotangent, segment_ids.reshape(1, tok))
+    return pl.pallas_call(
+        hand_over,
+        out_shape=shapes,
+        in_specs=[anywhere] * 3,
+        out_specs=(in_hbm,) * 3,
+        scratch_shapes=[dma((PIECES + 2,))],
+        compiler_params=pltpu.CompilerParams(vmem_limit_bytes=VMEM_BYTES),
+    )(*grads)
+
+
 def solution(mesh):
     placed = (
         P("section", "ctx", None),
@@ -146,8 +544,18 @@
         P("section", "ctx", None),
         P("ctx"),
     )
+    cycle_size = mesh.shape["ctx"]
+    pairs = mesh.shape["section"] == 2
+
+    def step(queries, keys, values, cotangent, segment_ids):
+        tok, width = keys.shape
+        halves = pairs and queries.shape[0] == 1 and tok % DH == 0 and width % (2 * DH) == 0
+        if halves:
+            return by_heads(cycle_size, queries, keys, values, cotangent, segment_ids)
+        return on_device(queries, keys, values, cotangent, segment_ids)
+
     return jax.shard_map(
-        on_device,
+        step,
         mesh=mesh,
         in_specs=placed,
         out_specs=(P("section", "ctx", None), P("ctx", "section"), P("ctx", "section")),

time: 106 us -> 49.2 us (0.46); the launches traced: 104 us -> 49.1 us
  Pallas kernels: 0 us -> 48.4 us
  starting transfers between devices: 29.9 us -> 0 us
  local copies, waits for them, and re-layouts: 21.4 us -> 0 us
  matrix products: 18.3 us -> 0 us
  waiting for transfers between devices: 16.5 us -> 0 us
  between operations: 14.5 us -> 0.64 us
  other arithmetic: 3.57 us -> 0 us
    pallas_call x0 -> x2, Pallas kernels: none -> 48.4 us  [the longest x1 29 us: by_heads(): pl.pallas_call(hand_over, out_shape=shapes, in_specs=[anywhere] * 3, out_...]
    ppermute x10 -> x0, starting transfers between devices: 29.8 us -> none  [shifted(): return lax.ppermute(shard, axis, pairs)]
    dot_general x18 -> x0, matrix products: 18.3 us -> none  [the longest x3 4.2 us: output_part(): jnp.einsum('grk,gkd->grd', probs_low, value_rows, preferred_element_type=...]
    reduce_scatter x2 -> x0, waiting for transfers between devices: 13.4 us -> none  [on_device(): lax.psum_scatter(summed, 'section', scatter_dimension=1, tiled=True)]
    reshape x6 -> x0, local copies, waits for them, and re-layouts: 8.23 us -> none  [the longest x2 3.31 us: on_device(): key_rows = key_block.reshape(tok_rows, groups, DH).transpose(1, 0, 2)]
    unnamed x42 -> x0, local copies, waits for them, and re-layouts: 6.14 us -> none
    ppermute x2 -> x0, local copies, waits for them, and re-layouts: 3.34 us -> none  [shifted(): return lax.ppermute(shard, axis, pairs)]
    ppermute x10 -> x0, waiting for transfers between devices: 3.1 us -> none  [shifted(): return lax.ppermute(shard, axis, pairs)]
  transfers between devices with their start and end apart: 12 -> 0, of which waited for: 4 -> 0; matrix products, arithmetic and copies ran while one was open for 31% -> 0% of each run, Pallas kernels for 0% -> 0%
where the time goes in v2:
time: 49.2 us; the launch traced here: 49.1 us
  Pallas kernels  48.4 us (98%)
  between operations  0.64 us (1%)
    pallas_call x1, Pallas kernels, by_heads(): pl.pallas_call(hand_over, out_shape=shapes, in_specs=[anywhere] * 3, out_...  29 us
    pallas_call x1, Pallas kernels, by_heads(): pl.pallas_call(functools.partial(kernel, cycle_size), out_shape=shapes, i...  19.5 us

profile of v2, /device:TPU:6, one launch (start us, length us, event | category | flops | bytes accessed | tf_op | source)
XLA Modules:
  0.0 49.1 jit_solution(2930234742138629222)
XLA Ops:
  0.6 19.5 %shard_map.76 = (bf16[1,128,2560]{2,1,0:T(8,128)(2,1)}, f32[128,256]{1,0:T(8,128)}, f32[128,256]{1,0:T(8,128)}) custom-call(bf16[1,128,2560]{2,1,0:T(8,128)(2,1)} %q_hbm.1, bf16[128,512]{1,0:T(8,128)(2,1)} %k_hbm.1, bf16[128,512]{1,0:T(8,128)(2,1)} %v_hbm.1, bf16[1,128,2560]{2,1,0:T(8,128)(2,1)} %g_hbm.1, s32[1,128]{1,0:T(1,128)} %bitcast.1), custom_call_target="tpu_custom_call" | custom-call | tf_op jit(solution)/shard_map/pallas_call | solution.py:496
  20.1 29.0 %shard_map.77 = (bf16[1,128,2560]{2,1,0:T(8,128)(2,1)}, f32[128,256]{1,0:T(8,128)}, f32[128,256]{1,0:T(8,128)}) custom-call(bf16[1,128,2560]{2,1,0:T(8,128)(2,1)} %get-tuple-element.6.dq_in, f32[128,256]{1,0:T(8,128)} %get-tuple-element.7.dk_in, f32[128,256]{1,0:T(8,128)} %get-tuple-element.8.dv_in), custom_call_target="tpu_custom_call" | custom-call | tf_op jit(solution)/shard_map/pallas_call | solution.py:529

commit v3 on v2

--- a/solution.py
+++ b/solution.py
@@ -463,16 +463,25 @@
                 parts[group][step].wait_send()
 
 
-def hand_over(dq_in, dk_in, dv_in, dq_out, dk_out, dv_out, sem):
+def hand_over(dq_in, dk_in, dv_in, dq_out, dk_out, dv_out, dq_buf, dk_buf, dv_buf, sem):
     piece = dq_in.shape[1] // PIECES
     cuts = [pl.ds(i * piece, piece) for i in range(PIECES)]
-    pairs = [(dq_in.at[:, cut], dq_out.at[:, cut]) for cut in cuts]
-    pairs += [(dk_in, dk_out), (dv_in, dv_out)]
-    copies = [pltpu.make_async_copy(*pair, sem.at[i]) for i, pair in enumerate(pairs)]
-    for copy in copies:
-        copy.start()
-    for copy in copies:
-        copy.wait()
+    ways = [(dq_in.at[:, cut], dq_buf.at[:, cut], dq_out.at[:, cut]) for cut in cuts]
+    ways += [(dk_in, dk_buf, dk_out), (dv_in, dv_buf, dv_out)]
+    copies = [
+        (
+            pltpu.make_async_copy(source, held, sem.at[0, i]),
+            pltpu.make_async_copy(held, target, sem.at[1, i]),
+        )
+        for i, (source, held, target) in enumerate(ways)
+    ]
+    for first, _ in copies:
+        first.start()
+    for first, second in copies:
+        first.wait()
+        second.start()
+    for _, second in copies:
+        second.wait()
 
 
 def by_heads(cycle_size, queries, keys, values, cotangent, segment_ids):
@@ -529,9 +538,10 @@
     return pl.pallas_call(
         hand_over,
         out_shape=shapes,
-        in_specs=[anywhere] * 3,
+        in_specs=[in_hbm] * 3,
         out_specs=(in_hbm,) * 3,
-        scratch_shapes=[dma((PIECES + 2,))],
+        scratch_shapes=[pltpu.VMEM(shape.shape, shape.dtype) for shape in shapes]
+        + [dma((2, PIECES + 2))],
         compiler_params=pltpu.CompilerParams(vmem_limit_bytes=VMEM_BYTES),
     )(*grads)
 

time: 49.2 us -> 22.3 us (0.45)
  Pallas kernels: 48.4 us -> 21.5 us
    pallas_call x1, Pallas kernels: 29 us -> 2.03 us  [by_heads(): pl.pallas_call(hand_over, out_shape=shapes, in_specs=[in_hbm] * 3, out_sp...]
where the time goes in v3:
time: 22.3 us; the launch traced here: 22.1 us
  Pallas kernels  21.5 us (96%)
  between operations  0.64 us (3%)
    pallas_call x1, Pallas kernels, by_heads(): pl.pallas_call(functools.partial(kernel, cycle_size), out_shape=shapes, i...  19.5 us
    pallas_call x1, Pallas kernels, by_heads(): pl.pallas_call(hand_over, out_shape=shapes, in_specs=[in_hbm] * 3, out_sp...  2.03 us

profile of v3, /device:TPU:6, one launch (start us, length us, event | category | flops | bytes accessed | tf_op | source)
XLA Modules:
  0.0 22.1 jit_solution(13705528125724244325)
XLA Ops:
  0.6 19.5 %shard_map.76 = (bf16[1,128,2560]{2,1,0:T(8,128)(2,1)}, f32[128,256]{1,0:T(8,128)}, f32[128,256]{1,0:T(8,128)}) custom-call(bf16[1,128,2560]{2,1,0:T(8,128)(2,1)} %q_hbm.1, bf16[128,512]{1,0:T(8,128)(2,1)} %k_hbm.1, bf16[128,512]{1,0:T(8,128)(2,1)} %v_hbm.1, bf16[1,128,2560]{2,1,0:T(8,128)(2,1)} %g_hbm.1, s32[1,128]{1,0:T(1,128)} %bitcast.1), custom_call_target="tpu_custom_call" | custom-call | tf_op jit(solution)/shard_map/pallas_call | solution.py:505
  20.1 2.0 %shard_map.77 = (bf16[1,128,2560]{2,1,0:T(8,128)(2,1)}, f32[128,256]{1,0:T(8,128)}, f32[128,256]{1,0:T(8,128)}) custom-call(bf16[1,128,2560]{2,1,0:T(8,128)(2,1)} %get-tuple-element.6.dq_in, f32[128,256]{1,0:T(8,128)} %get-tuple-element.7.dk_in, f32[128,256]{1,0:T(8,128)} %get-tuple-element.8.dv_in), custom_call_target="tpu_custom_call" | custom-call | tf_op jit(solution)/shard_map/pallas_call | solution.py:538

commit v4 on v3

--- a/solution.py
+++ b/solution.py
@@ -171,6 +171,8 @@
     v_buf,
     seg_buf,
     bias,
+    s_own,
+    gp_own,
     s_buf,
     gp_buf,
     p_buf,
@@ -323,53 +325,64 @@
     def stacked(buf, slot, group):
         return jnp.concatenate([buf[slot, group, :, head_cols(h)] for h in range(ratio)], 0)
 
-    def products(step, slot, group):
-        s_buf[group, slot, block(step), :] = dot(
-            k_buf[group, block(step), :], stacked(q_buf, slot, group), 1, 1
-        )
-        gp_buf[group, slot, block(step), :] = dot(
-            v_buf[group, block(step), :], stacked(g_buf, slot, group), 1, 1
-        )
-
-    def mask(step):
-        key_seg = jnp.broadcast_to(seg_buf[step].astype(jnp.float32), (tok, tok)).T
-        row_seg = seg_buf[0].astype(jnp.float32)
-        allowed = key_seg == row_seg
-        if step == 0:
-            key_at = lax.broadcasted_iota(jnp.int32, (tok, tok), 0)
-            row_at = lax.broadcasted_iota(jnp.int32, (tok, tok), 1)
-            allowed = allowed & (key_at <= row_at)
-        bias[block(step), :] = jnp.where(allowed, 0.0, -1e30)
-
-    def probabilities(group, slot):
-        for head in range(ratio):
-            cols = slice(head * tok, (head + 1) * tok)
-            scores = s_buf[group, slot, :, cols] * (scale * LOG2E) + bias[...]
-            exps = jnp.exp2(scores - jnp.max(scores, 0, keepdims=True))
-            grad_probs = gp_buf[group, slot, :, cols]
-            inverse = 1.0 / jnp.sum(exps, 0, keepdims=True)
-            probs = exps * inverse
-            row_dot = jnp.sum(probs * grad_probs, 0, keepdims=True)
-            scaled = probs * (grad_probs - row_dot) * scale
-            at = slice(slot * rows + head * tok, slot * rows + (head + 1) * tok)
-            p_buf[group, :, at] = probs.astype(jnp.bfloat16)
-            ds_buf[group, :, at] = scaled.astype(jnp.bfloat16)
-
     def all_rows(buf, group):
         return jnp.concatenate([stacked(buf, 0, group), stacked(buf, 1, group)], 0)
 
-    def key_value_grads(step, group):
+    def own_products(slot, group):
+        at = slice(slot * rows, (slot + 1) * rows)
+        s_own[group, :, at] = dot(k_buf[group, block(0), :], stacked(q_buf, slot, group), 1, 1)
+        gp_own[group, :, at] = dot(v_buf[group, block(0), :], stacked(g_buf, slot, group), 1, 1)
+
+    key_at = lax.broadcasted_iota(jnp.int32, (tok, tok), 0)
+    row_at = lax.broadcasted_iota(jnp.int32, (tok, tok), 1)
+    is_own = key_at <= row_at
+
+    def key_segments(step):
+        return jnp.broadcast_to(seg_buf[step].astype(jnp.float32), (tok, tok)).T
+
+    def fill_bias():
+        last = shards - 1
+        row_seg = seg_buf[0].astype(jnp.float32)
+        edge = jnp.where(is_own, key_segments(0), key_segments(last))
+        bias[last * tok :, :] = jnp.where(edge == row_seg, 0.0, -1e30)
+        for step in range(1, last):
+            bias[block(step), :] = jnp.where(key_segments(step) == row_seg, 0.0, -1e30)
+
+    inner = slice(tok, None)
+
+    def probabilities(group):
+        span = 2 * rows
+        for start in range(0, span, tok):
+            cols = slice(start, start + tok)
+            edge_s = jnp.where(is_own, s_own[group, :, cols], s_buf[group, :tok, cols])
+            edge_gp = jnp.where(is_own, gp_own[group, :, cols], gp_buf[group, :tok, cols])
+            grad_probs = jnp.concatenate([gp_buf[group, inner, cols], edge_gp], 0)
+            scores = jnp.concatenate([s_buf[group, inner, cols], edge_s], 0)
+            scores = scores * (scale * LOG2E) + bias[inner, :]
+            exps = jnp.exp2(scores - jnp.max(scores, 0, keepdims=True))
+            total = jnp.sum(exps, 0, keepdims=True)
+            row_dot = jnp.sum(exps * grad_probs, 0, keepdims=True) / total
+            probs = exps * (1.0 / total)
+            scaled = probs * (grad_probs - row_dot)
+            for target, value in ((p_buf, probs), (ds_buf, scaled)):
+                edge = value[-tok:]
+                target[group, inner, cols] = jnp.concatenate(
+                    [value[:-tok], jnp.where(is_own, edge, 0.0)], 0
+                ).astype(jnp.bfloat16)
+                target[group, :tok, cols] = jnp.where(is_own, 0.0, edge).astype(jnp.bfloat16)
+
+    def key_value_grads(at, group):
         return (
-            dot(ds_buf[group, block(step), :], all_rows(q_buf, group), 1, 0),
-            dot(p_buf[group, block(step), :], all_rows(g_buf, group), 1, 0),
+            dot(ds_buf[group, at, :], all_rows(q_buf, group), 1, 0) * scale,
+            dot(p_buf[group, at, :], all_rows(g_buf, group), 1, 0),
         )
 
     def query_grads(group, slot):
         flipped = dot(k_buf[group], ds_buf[group, :, slot * rows : (slot + 1) * rows], 0, 0)
         for head in range(ratio):
-            dq_buf[slot, group, :, head_cols(head)] = flipped[
-                :, head * tok : (head + 1) * tok
-            ].T.astype(jnp.bfloat16)
+            dq_buf[slot, group, :, head_cols(head)] = (
+                flipped[:, head * tok : (head + 1) * tok].T * scale
+            ).astype(jnp.bfloat16)
 
     def part_copy(step, group):
         return pltpu.make_async_remote_copy(
@@ -394,15 +407,15 @@
     ]
 
     own_seg.wait()
-    mask(0)
     for group in range(groups):
         for copy in own[group]:
             copy.wait()
-        products(0, 0, group)
+        own_products(0, group)
     for group in range(groups):
         for copy in pair[group]:
             copy.wait_recv()
-        products(0, 1, group)
+        own_products(1, group)
+    far = slice(0, DOC_SHARDS * tok)
     for group in range(groups):
         for step in steps:
 
@@ -413,26 +426,29 @@
                 for copy in near[step][group]:
                     copy.wait_recv()
 
-            if group == 0:
-                mask(step)
-            products(step, 0, group)
-            products(step, 1, group)
-        probabilities(group, 0)
-        probabilities(group, 1)
+        if group == 0:
+            fill_bias()
+        s_buf[group] = dot(k_buf[group, far, :], all_rows(q_buf, group), 1, 1)
+        gp_buf[group] = dot(v_buf[group, far, :], all_rows(g_buf, group), 1, 1)
+        probabilities(group)
+        grad_key, grad_value = key_value_grads(far, group)
+        for step in steps:
+            part[group, step - 1, 0] = grad_key[block(step)].astype(jnp.bfloat16)
+            part[group, step - 1, 1] = grad_value[block(step)].astype(jnp.bfloat16)
         for step in reversed(steps):
-            grad_key, grad_value = key_value_grads(step, group)
-            part[group, step - 1, 0] = grad_key.astype(jnp.bfloat16)
-            part[group, step - 1, 1] = grad_value.astype(jnp.bfloat16)
 
             @pl.when(me >= step)
             def _(step=step, group=group):
                 parts[group][step].start()
 
+    for group in range(groups):
         query_grads(group, 1)
         query_send[group].start()
+    for group in range(groups):
         query_grads(group, 0)
         query_keep[group].start()
-        grad_key, grad_value = key_value_grads(0, group)
+    for group in range(groups):
+        grad_key, grad_value = key_value_grads(block(0), group)
         dk_ref[:, head_cols(group)] = grad_key
         dv_ref[:, head_cols(group)] = grad_value
     for group in range(groups):
@@ -514,8 +530,10 @@
             pltpu.VMEM((groups, window, DH), bf16),
             pltpu.VMEM((DOC_SHARDS + 1, 1, tok), jnp.int32),
             pltpu.VMEM((window, tok), f32),
-            pltpu.VMEM((groups, 2, window, rows), f32),
-            pltpu.VMEM((groups, 2, window, rows), f32),
+            pltpu.VMEM((groups, tok, 2 * rows), f32),
+            pltpu.VMEM((groups, tok, 2 * rows), f32),
+            pltpu.VMEM((groups, window - tok, 2 * rows), f32),
+            pltpu.VMEM((groups, window - tok, 2 * rows), f32),
             pltpu.VMEM((groups, window, 2 * rows), bf16),
             pltpu.VMEM((groups, window, 2 * rows), bf16),
             pltpu.VMEM((2, groups, tok, half // groups), bf16),

time: 22.3 us -> 21.1 us (0.946)
  Pallas kernels: 21.5 us -> 20.3 us
    pallas_call x1, Pallas kernels: 19.5 us -> 18.3 us  [by_heads(): pl.pallas_call(functools.partial(kernel, cycle_size), out_shape=shapes, i...]
where the time goes in v4:
time: 21.1 us; the launch traced here: 20.9 us
  Pallas kernels  20.3 us (96%)
  between operations  0.64 us (3%)
    pallas_call x1, Pallas kernels, by_heads(): pl.pallas_call(functools.partial(kernel, cycle_size), out_shape=shapes, i...  18.3 us
    pallas_call x1, Pallas kernels, by_heads(): pl.pallas_call(hand_over, out_shape=shapes, in_specs=[in_hbm] * 3, out_sp...  2.03 us

profile of v4, /device:TPU:6, one launch (start us, length us, event | category | flops | bytes accessed | tf_op | source)
XLA Modules:
  0.0 20.9 jit_solution(9043462305954263689)
XLA Ops:
  0.6 18.3 %shard_map.76 = (bf16[1,128,2560]{2,1,0:T(8,128)(2,1)}, f32[128,256]{1,0:T(8,128)}, f32[128,256]{1,0:T(8,128)}) custom-call(bf16[1,128,2560]{2,1,0:T(8,128)(2,1)} %q_hbm.1, bf16[128,512]{1,0:T(8,128)(2,1)} %k_hbm.1, bf16[128,512]{1,0:T(8,128)(2,1)} %v_hbm.1, bf16[1,128,2560]{2,1,0:T(8,128)(2,1)} %g_hbm.1, s32[1,128]{1,0:T(1,128)} %bitcast.1), custom_call_target="tpu_custom_call" | custom-call | tf_op jit(solution)/shard_map/pallas_call | solution.py:521
  18.9 2.0 %shard_map.77 = (bf16[1,128,2560]{2,1,0:T(8,128)(2,1)}, f32[128,256]{1,0:T(8,128)}, f32[128,256]{1,0:T(8,128)}) custom-call(bf16[1,128,2560]{2,1,0:T(8,128)(2,1)} %get-tuple-element.6.dq_in, f32[128,256]{1,0:T(8,128)} %get-tuple-element.7.dk_in, f32[128,256]{1,0:T(8,128)} %get-tuple-element.8.dv_in), custom_call_target="tpu_custom_call" | custom-call | tf_op jit(solution)/shard_map/pallas_call | solution.py:556

commit v5 on v4

--- a/solution.py
+++ b/solution.py
@@ -306,16 +306,28 @@
         ]
         for group in range(groups)
     ]
-    for group in range(groups):
+    def send_near(group):
         for step in reversed(steps):
 
             @pl.when(me + step < cycle_size)
-            def _(step=step, group=group):
+            def _(step=step):
                 if group == 0:
                     near_seg[step].start()
                 for copy in near[step][group]:
                     copy.start()
 
+    def near_sent(group):
+        for step in steps:
+
+            @pl.when(me + step < cycle_size)
+            def _(step=step):
+                if group == 0:
+                    near_seg[step].wait_send()
+                for copy in near[step][group]:
+                    copy.wait_send()
+
+    send_near(0)
+    for group in range(groups):
         for copy in pair[group]:
             copy.start()
 
@@ -410,6 +422,9 @@
     for group in range(groups):
         for copy in own[group]:
             copy.wait()
+        if group > 0:
+            near_sent(group - 1)
+            send_near(group)
         own_products(0, group)
     for group in range(groups):
         for copy in pair[group]:
@@ -467,16 +482,11 @@
             copy.wait_send()
         for step in steps:
 
-            @pl.when(me + step < cycle_size)
-            def _(step=step, group=group):
-                if group == 0:
-                    near_seg[step].wait_send()
-                for copy in near[step][group]:
-                    copy.wait_send()
-
             @pl.when(me >= step)
             def _(step=step, group=group):
                 parts[group][step].wait_send()
+
+    near_sent(groups - 1)
 
 
 def hand_over(dq_in, dk_in, dv_in, dq_out, dk_out, dv_out, dq_buf, dk_buf, dv_buf, sem):

time: 21.1 us -> 21 us (level)
  no operation moved by 1% of the time
where the time goes in v5:
time: 21 us; the launch traced here: 20.9 us
  Pallas kernels  20.2 us (96%)
  between operations  0.64 us (3%)
    pallas_call x1, Pallas kernels, by_heads(): pl.pallas_call(functools.partial(kernel, cycle_size), out_shape=shapes, i...  18.2 us
    pallas_call x1, Pallas kernels, by_heads(): pl.pallas_call(hand_over, out_shape=shapes, in_specs=[in_hbm] * 3, out_sp...  2.03 us

profile of v5, /device:TPU:6, one launch (start us, length us, event | category | flops | bytes accessed | tf_op | source)
XLA Modules:
  0.0 20.9 jit_solution(1942762702891235672)
XLA Ops:
  0.6 18.2 %shard_map.76 = (bf16[1,128,2560]{2,1,0:T(8,128)(2,1)}, f32[128,256]{1,0:T(8,128)}, f32[128,256]{1,0:T(8,128)}) custom-call(bf16[1,128,2560]{2,1,0:T(8,128)(2,1)} %q_hbm.1, bf16[128,512]{1,0:T(8,128)(2,1)} %k_hbm.1, bf16[128,512]{1,0:T(8,128)(2,1)} %v_hbm.1, bf16[1,128,2560]{2,1,0:T(8,128)(2,1)} %g_hbm.1, s32[1,128]{1,0:T(1,128)} %bitcast.1), custom_call_target="tpu_custom_call" | custom-call | tf_op jit(solution)/shard_map/pallas_call | solution.py:531
  18.8 2.0 %shard_map.77 = (bf16[1,128,2560]{2,1,0:T(8,128)(2,1)}, f32[128,256]{1,0:T(8,128)}, f32[128,256]{1,0:T(8,128)}) custom-call(bf16[1,128,2560]{2,1,0:T(8,128)(2,1)} %get-tuple-element.6.dq_in, f32[128,256]{1,0:T(8,128)} %get-tuple-element.7.dk_in, f32[128,256]{1,0:T(8,128)} %get-tuple-element.8.dv_in), custom_call_target="tpu_custom_call" | custom-call | tf_op jit(solution)/shard_map/pallas_call | solution.py:566

commit v6 on v5

--- a/solution.py
+++ b/solution.py
@@ -162,7 +162,7 @@
     v_hbm,
     g_hbm,
     seg_hbm,
-    dq_hbm,
+    dq_ref,
     dk_ref,
     dv_ref,
     q_buf,
@@ -392,9 +392,13 @@
     def query_grads(group, slot):
         flipped = dot(k_buf[group], ds_buf[group, :, slot * rows : (slot + 1) * rows], 0, 0)
         for head in range(ratio):
-            dq_buf[slot, group, :, head_cols(head)] = (
-                flipped[:, head * tok : (head + 1) * tok].T * scale
-            ).astype(jnp.bfloat16)
+            grad_query = flipped[:, head * tok : (head + 1) * tok].T * scale
+            grad_query = grad_query.astype(jnp.bfloat16)
+            if slot == 0:
+                start = (core * groups + group) * share + head * DH
+                dq_ref[0, :, pl.ds(pl.multiple_of(start, DH), DH)] = grad_query
+            else:
+                dq_buf[group, :, head_cols(head)] = grad_query
 
     def part_copy(step, group):
         return pltpu.make_async_remote_copy(
@@ -408,16 +412,9 @@
 
     parts = [{step: part_copy(step, group) for step in steps} for group in range(groups)]
     query_send = [
-        pair_copy(dq_buf.at[1, group], dq_hbm.at[0, :, query_cols(core, group)], group, 2)
+        pair_copy(dq_buf.at[group], dq_ref.at[0, :, query_cols(core, group)], group, 2)
         for group in range(groups)
     ]
-    query_keep = [
-        pltpu.make_async_copy(
-            dq_buf.at[0, group], dq_hbm.at[0, :, query_cols(core, group)], local_sem.at[group, 4]
-        )
-        for group in range(groups)
-    ]
-
     own_seg.wait()
     for group in range(groups):
         for copy in own[group]:
@@ -461,7 +458,6 @@
         query_send[group].start()
     for group in range(groups):
         query_grads(group, 0)
-        query_keep[group].start()
     for group in range(groups):
         grad_key, grad_value = key_value_grads(block(0), group)
         dk_ref[:, head_cols(group)] = grad_key
@@ -476,7 +472,6 @@
                 dv_ref[:, head_cols(group)] += got[group, step - 1, 1].astype(jnp.float32)
 
     for group in range(groups):
-        query_keep[group].wait()
         query_send[group].wait()
         for copy in pair[group]:
             copy.wait_send()
@@ -489,25 +484,16 @@
     near_sent(groups - 1)
 
 
-def hand_over(dq_in, dk_in, dv_in, dq_out, dk_out, dv_out, dq_buf, dk_buf, dv_buf, sem):
+def hand_over(dq_in, dk_in, dv_in, dq_out, dk_out, dv_out, sem):
     piece = dq_in.shape[1] // PIECES
     cuts = [pl.ds(i * piece, piece) for i in range(PIECES)]
-    ways = [(dq_in.at[:, cut], dq_buf.at[:, cut], dq_out.at[:, cut]) for cut in cuts]
-    ways += [(dk_in, dk_buf, dk_out), (dv_in, dv_buf, dv_out)]
-    copies = [
-        (
-            pltpu.make_async_copy(source, held, sem.at[0, i]),
-            pltpu.make_async_copy(held, target, sem.at[1, i]),
-        )
-        for i, (source, held, target) in enumerate(ways)
-    ]
-    for first, _ in copies:
-        first.start()
-    for first, second in copies:
-        first.wait()
-        second.start()
-    for _, second in copies:
-        second.wait()
+    pairs = [(dq_in.at[:, cut], dq_out.at[:, cut]) for cut in cuts]
+    pairs += [(dk_in, dk_out), (dv_in, dv_out)]
+    copies = [pltpu.make_async_copy(*pair, sem.at[i]) for i, pair in enumerate(pairs)]
+    for copy in copies:
+        copy.start()
+    for copy in copies:
+        copy.wait()
 
 
 def by_heads(cycle_size, queries, keys, values, cotangent, segment_ids):
@@ -530,9 +516,9 @@
     )
     grads = pl.pallas_call(
         functools.partial(kernel, cycle_size),
-        out_shape=shapes,
+        out_shape=tuple(pltpu.VMEM(shape.shape, shape.dtype) for shape in shapes),
         in_specs=[in_hbm] * 5,
-        out_specs=(anywhere, in_vmem, in_vmem),
+        out_specs=(in_vmem,) * 3,
         scratch_shapes=[
             pltpu.VMEM((2, groups, tok, half // groups), bf16),
             pltpu.VMEM((2, groups, tok, half // groups), bf16),
@@ -546,7 +532,7 @@
             pltpu.VMEM((groups, window - tok, 2 * rows), f32),
             pltpu.VMEM((groups, window, 2 * rows), bf16),
             pltpu.VMEM((groups, window, 2 * rows), bf16),
-            pltpu.VMEM((2, groups, tok, half // groups), bf16),
+            pltpu.VMEM((groups, tok, half // groups), bf16),
             pltpu.VMEM((groups, DOC_SHARDS, 2, tok, DH), bf16),
             pltpu.VMEM((groups, DOC_SHARDS, 2, tok, DH), bf16),
             dma((groups + 1, 5)),
@@ -566,11 +552,10 @@
     return pl.pallas_call(
         hand_over,
         out_shape=shapes,
-        in_specs=[in_hbm] * 3,
+        in_specs=[in_vmem] * 3,
         out_specs=(in_hbm,) * 3,
-        scratch_shapes=[pltpu.VMEM(shape.shape, shape.dtype) for shape in shapes]
-        + [dma((2, PIECES + 2))],
-        compiler_params=pltpu.CompilerParams(vmem_limit_bytes=VMEM_BYTES),
+        scratch_shapes=[dma((PIECES + 2,))],
+        compiler_params=pltpu.CompilerParams(vmem_limit_bytes=8 << 20),
     )(*grads)
 
 

time: 21 us -> 19.2 us (0.914)
  Pallas kernels: 20.2 us -> 18.4 us
    pallas_call x2, Pallas kernels: 20.2 us -> 18.4 us  [the longest x1 17.5 us: by_heads(): pl.pallas_call(functools.partial(kernel, cycle_size), out_shape=tuple((pl...]
where the time goes in v6:
time: 19.2 us; the launch traced here: 19.1 us
  Pallas kernels  18.4 us (96%)
  between operations  0.64 us (3%)
    pallas_call x1, Pallas kernels, by_heads(): pl.pallas_call(functools.partial(kernel, cycle_size), out_shape=tuple((pl...  17.5 us
    pallas_call x1, Pallas kernels, by_heads(): pl.pallas_call(hand_over, out_shape=shapes, in_specs=[in_vmem] * 3, out_s...  0.97 us

profile of v6, /device:TPU:6, one launch (start us, length us, event | category | flops | bytes accessed | tf_op | source)
XLA Modules:
  0.0 19.1 jit_solution(8712241762435106081)
XLA Ops:
  0.6 17.5 %shard_map.76 = (bf16[1,128,2560]{2,1,0:T(8,128)(2,1)S(1)}, f32[128,256]{1,0:T(8,128)S(1)}, f32[128,256]{1,0:T(8,128)S(1)}) custom-call(bf16[1,128,2560]{2,1,0:T(8,128)(2,1)} %q_hbm.1, bf16[128,512]{1,0:T(8,128)(2,1)} %k_hbm.1, bf16[128,512]{1,0:T(8,128)(2,1)} %v_hbm.1, bf16[1,128,2560]{2,1,0:T(8,128)(2,1)} %g_hbm.1, s32[1,128]{1,0:T(1,128)} %bitcast.1), custom_call_target="tpu_custom_call" | custom-call | tf_op jit(solution)/shard_map/pallas_call | solution.py:517
  18.1 1.0 %shard_map.77 = (bf16[1,128,2560]{2,1,0:T(8,128)(2,1)}, f32[128,256]{1,0:T(8,128)}, f32[128,256]{1,0:T(8,128)}) custom-call(bf16[1,128,2560]{2,1,0:T(8,128)(2,1)S(1)} %get-tuple-element.6.dq_in, f32[128,256]{1,0:T(8,128)S(1)} %get-tuple-element.7.dk_in, f32[128,256]{1,0:T(8,128)S(1)} %get-tuple-element.8.dv_in), custom_call_target="tpu_custom_call" | custom-call | tf_op jit(solution)/shard_map/pallas_call | solution.py:552

commit v7 on v6

--- a/solution.py
+++ b/solution.py
@@ -307,14 +307,14 @@
         for group in range(groups)
     ]
     def send_near(group):
-        for step in reversed(steps):
-
-            @pl.when(me + step < cycle_size)
-            def _(step=step):
-                if group == 0:
-                    near_seg[step].start()
-                for copy in near[step][group]:
-                    copy.start()
+        for which in range(2):
+            for step in reversed(steps):
+
+                @pl.when(me + step < cycle_size)
+                def _(step=step, which=which):
+                    if group == 0 and which == 0:
+                        near_seg[step].start()
+                    near[step][group][which].start()
 
     def near_sent(group):
         for step in steps:
@@ -362,32 +362,38 @@
 
     inner = slice(tok, None)
 
+    def store_tiles(target, group, cols, value):
+        edge = value[-tok:]
+        target[group, inner, cols] = jnp.concatenate(
+            [value[:-tok], jnp.where(is_own, edge, 0.0)], 0
+        ).astype(jnp.bfloat16)
+        target[group, :tok, cols] = jnp.where(is_own, 0.0, edge).astype(jnp.bfloat16)
+
     def probabilities(group):
-        span = 2 * rows
-        for start in range(0, span, tok):
+        for start in range(0, 2 * rows, tok):
             cols = slice(start, start + tok)
-            edge_s = jnp.where(is_own, s_own[group, :, cols], s_buf[group, :tok, cols])
-            edge_gp = jnp.where(is_own, gp_own[group, :, cols], gp_buf[group, :tok, cols])
-            grad_probs = jnp.concatenate([gp_buf[group, inner, cols], edge_gp], 0)
-            scores = jnp.concatenate([s_buf[group, inner, cols], edge_s], 0)
+            edge = jnp.where(is_own, s_own[group, :, cols], s_buf[group, :tok, cols])
+            scores = jnp.concatenate([s_buf[group, inner, cols], edge], 0)
             scores = scores * (scale * LOG2E) + bias[inner, :]
             exps = jnp.exp2(scores - jnp.max(scores, 0, keepdims=True))
-            total = jnp.sum(exps, 0, keepdims=True)
-            row_dot = jnp.sum(exps * grad_probs, 0, keepdims=True) / total
-            probs = exps * (1.0 / total)
-            scaled = probs * (grad_probs - row_dot)
-            for target, value in ((p_buf, probs), (ds_buf, scaled)):
-                edge = value[-tok:]
-                target[group, inner, cols] = jnp.concatenate(
-                    [value[:-tok], jnp.where(is_own, edge, 0.0)], 0
-                ).astype(jnp.bfloat16)
-                target[group, :tok, cols] = jnp.where(is_own, 0.0, edge).astype(jnp.bfloat16)
-
-    def key_value_grads(at, group):
-        return (
-            dot(ds_buf[group, at, :], all_rows(q_buf, group), 1, 0) * scale,
-            dot(p_buf[group, at, :], all_rows(g_buf, group), 1, 0),
-        )
+            probs = exps * (1.0 / jnp.sum(exps, 0, keepdims=True))
+            s_buf[group, :, cols] = probs
+            store_tiles(p_buf, group, cols, probs)
+
+    def score_grads(group):
+        for start in range(0, 2 * rows, tok):
+            cols = slice(start, start + tok)
+            edge = jnp.where(is_own, gp_own[group, :, cols], gp_buf[group, :tok, cols])
+            grad_probs = jnp.concatenate([gp_buf[group, inner, cols], edge], 0)
+            probs = s_buf[group, :, cols]
+            row_dot = jnp.sum(probs * grad_probs, 0, keepdims=True)
+            store_tiles(ds_buf, group, cols, probs * (grad_probs - row_dot))
+
+    def key_grads(at, group):
+        return dot(ds_buf[group, at, :], all_rows(q_buf, group), 1, 0) * scale
+
+    def value_grads(at, group):
+        return dot(p_buf[group, at, :], all_rows(g_buf, group), 1, 0)
 
     def query_grads(group, slot):
         flipped = dot(k_buf[group], ds_buf[group, :, slot * rows : (slot + 1) * rows], 0, 0)
@@ -400,17 +406,39 @@
             else:
                 dq_buf[group, :, head_cols(head)] = grad_query
 
-    def part_copy(step, group):
+    def part_copy(step, group, which):
         return pltpu.make_async_remote_copy(
-            src_ref=part.at[group, step - 1],
-            dst_ref=got.at[group, step - 1],
-            send_sem=part_send.at[group, step - 1],
-            recv_sem=part_recv.at[group, step - 1],
+            src_ref=part.at[group, step - 1, which],
+            dst_ref=got.at[group, step - 1, which],
+            send_sem=part_send.at[group, step - 1, which],
+            recv_sem=part_recv.at[group, step - 1, which],
             device_id={"ctx": me - step},
             device_id_type=MESH,
         )
 
-    parts = [{step: part_copy(step, group) for step in steps} for group in range(groups)]
+    parts = [
+        {step: [part_copy(step, group, which) for which in range(2)] for step in steps}
+        for group in range(groups)
+    ]
+
+    def send_part(group, which, grad):
+        for step in steps:
+            part[group, step - 1, which] = grad[block(step)].astype(jnp.bfloat16)
+        for step in reversed(steps):
+
+            @pl.when(me >= step)
+            def _(step=step):
+                parts[group][step][which].start()
+
+    def near_arrived(group, which):
+        for step in steps:
+
+            @pl.when(me >= step)
+            def _(step=step):
+                if group == 0 and which == 0:
+                    near_seg[step].wait_recv()
+                near[step][group][which].wait_recv()
+
     query_send = [
         pair_copy(dq_buf.at[group], dq_ref.at[0, :, query_cols(core, group)], group, 2)
         for group in range(groups)
@@ -429,47 +457,32 @@
         own_products(1, group)
     far = slice(0, DOC_SHARDS * tok)
     for group in range(groups):
-        for step in steps:
-
-            @pl.when(me >= step)
-            def _(step=step, group=group):
-                if group == 0:
-                    near_seg[step].wait_recv()
-                for copy in near[step][group]:
-                    copy.wait_recv()
-
+        near_arrived(group, 0)
         if group == 0:
             fill_bias()
         s_buf[group] = dot(k_buf[group, far, :], all_rows(q_buf, group), 1, 1)
+        probabilities(group)
+        send_part(group, 1, value_grads(far, group))
+        near_arrived(group, 1)
         gp_buf[group] = dot(v_buf[group, far, :], all_rows(g_buf, group), 1, 1)
-        probabilities(group)
-        grad_key, grad_value = key_value_grads(far, group)
-        for step in steps:
-            part[group, step - 1, 0] = grad_key[block(step)].astype(jnp.bfloat16)
-            part[group, step - 1, 1] = grad_value[block(step)].astype(jnp.bfloat16)
-        for step in reversed(steps):
-
-            @pl.when(me >= step)
-            def _(step=step, group=group):
-                parts[group][step].start()
-
+        score_grads(group)
+        send_part(group, 0, key_grads(far, group))
     for group in range(groups):
         query_grads(group, 1)
         query_send[group].start()
     for group in range(groups):
         query_grads(group, 0)
-    for group in range(groups):
-        grad_key, grad_value = key_value_grads(block(0), group)
-        dk_ref[:, head_cols(group)] = grad_key
-        dv_ref[:, head_cols(group)] = grad_value
-    for group in range(groups):
-        for step in steps:
-
-            @pl.when(me + step < cycle_size)
-            def _(step=step, group=group):
-                parts[group][step].wait_recv()
-                dk_ref[:, head_cols(group)] += got[group, step - 1, 0].astype(jnp.float32)
-                dv_ref[:, head_cols(group)] += got[group, step - 1, 1].astype(jnp.float32)
+        dk_ref[:, head_cols(group)] = key_grads(block(0), group)
+        dv_ref[:, head_cols(group)] = value_grads(block(0), group)
+    for group in range(groups):
+        for which, target in ((1, dv_ref), (0, dk_ref)):
+            for step in steps:
+
+                @pl.when(me + step < cycle_size)
+                def _(step=step, group=group, which=which, target=target):
+                    parts[group][step][which].wait_recv()
+                    more = got[group, step - 1, which].astype(jnp.float32)
+                    target[:, head_cols(group)] += more
 
     for group in range(groups):
         query_send[group].wait()
@@ -479,7 +492,8 @@
 
             @pl.when(me >= step)
             def _(step=step, group=group):
-                parts[group][step].wait_send()
+                for copy in parts[group][step]:
+                    copy.wait_send()
 
     near_sent(groups - 1)
 
@@ -542,8 +556,8 @@
             dma((DOC_SHARDS,)),
             dma((DOC_SHARDS, groups, 2)),
             dma((DOC_SHARDS, groups, 2)),
-            dma((groups, DOC_SHARDS)),
-            dma((groups, DOC_SHARDS)),
+            dma((groups, DOC_SHARDS, 2)),
+            dma((groups, DOC_SHARDS, 2)),
         ],
         compiler_params=pltpu.CompilerParams(
             collective_id=0, has_side_effects=True, vmem_limit_bytes=VMEM_BYTES

time: 19.2 us -> 18.1 us (0.943)
  Pallas kernels: 18.4 us -> 17.2 us
    pallas_call x1, Pallas kernels: 17.5 us -> 16.2 us  [by_heads(): pl.pallas_call(functools.partial(kernel, cycle_size), out_shape=tuple((pl...]
where the time goes in v7:
time: 18.1 us; the launch traced here: 17.8 us
  Pallas kernels  17.2 us (95%)
  between operations  0.64 us (4%)
    pallas_call x1, Pallas kernels, by_heads(): pl.pallas_call(functools.partial(kernel, cycle_size), out_shape=tuple((pl...  16.2 us
    pallas_call x1, Pallas kernels, by_heads(): pl.pallas_call(hand_over, out_shape=shapes, in_specs=[in_vmem] * 3, out_s...  0.97 us

profile of v7, /device:TPU:6, one launch (start us, length us, event | category | flops | bytes accessed | tf_op | source)
XLA Modules:
  0.0 17.8 jit_solution(5523183546575938093)
XLA Ops:
  0.6 16.2 %shard_map.76 = (bf16[1,128,2560]{2,1,0:T(8,128)(2,1)S(1)}, f32[128,256]{1,0:T(8,128)S(1)}, f32[128,256]{1,0:T(8,128)S(1)}) custom-call(bf16[1,128,2560]{2,1,0:T(8,128)(2,1)} %q_hbm.1, bf16[128,512]{1,0:T(8,128)(2,1)} %k_hbm.1, bf16[128,512]{1,0:T(8,128)(2,1)} %v_hbm.1, bf16[1,128,2560]{2,1,0:T(8,128)(2,1)} %g_hbm.1, s32[1,128]{1,0:T(1,128)} %bitcast.1), custom_call_target="tpu_custom_call" | custom-call | tf_op jit(solution)/shard_map/pallas_call | solution.py:531
  16.9 1.0 %shard_map.77 = (bf16[1,128,2560]{2,1,0:T(8,128)(2,1)}, f32[128,256]{1,0:T(8,128)}, f32[128,256]{1,0:T(8,128)}) custom-call(bf16[1,128,2560]{2,1,0:T(8,128)(2,1)S(1)} %get-tuple-element.6.dq_in, f32[128,256]{1,0:T(8,128)S(1)} %get-tuple-element.7.dk_in, f32[128,256]{1,0:T(8,128)S(1)} %get-tuple-element.8.dv_in), custom_call_target="tpu_custom_call" | custom-call | tf_op jit(solution)/shard_map/pallas_call | solution.py:566

commit v8 on v7

--- a/solution.py
+++ b/solution.py
@@ -326,8 +326,8 @@
                 for copy in near[step][group]:
                     copy.wait_send()
 
-    send_near(0)
-    for group in range(groups):
+    for group in range(groups):
+        send_near(group)
         for copy in pair[group]:
             copy.start()
 
@@ -447,9 +447,6 @@
     for group in range(groups):
         for copy in own[group]:
             copy.wait()
-        if group > 0:
-            near_sent(group - 1)
-            send_near(group)
         own_products(0, group)
     for group in range(groups):
         for copy in pair[group]:
@@ -495,7 +492,8 @@
                 for copy in parts[group][step]:
                     copy.wait_send()
 
-    near_sent(groups - 1)
+    for group in range(groups):
+        near_sent(group)
 
 
 def hand_over(dq_in, dk_in, dv_in, dq_out, dk_out, dv_out, sem):

time: 18.1 us -> 18.4 us (1.017)
  the two profiles are of different devices: /device:TPU:6 before, /device:TPU:0 now
where the time goes in v8:
time: 18.4 us; the launch traced here: 18.3 us
  Pallas kernels  17.7 us (96%)
  between operations  0.64 us (3%)
    pallas_call x1, Pallas kernels, by_heads(): pl.pallas_call(functools.partial(kernel, cycle_size), out_shape=tuple((pl...  16.7 us
    pallas_call x1, Pallas kernels, by_heads(): pl.pallas_call(hand_over, out_shape=shapes, in_specs=[in_vmem] * 3, out_s...  0.97 us

profile of v8, /device:TPU:0, one launch (start us, length us, event | category | flops | bytes accessed | tf_op | source)
XLA Modules:
  0.0 18.3 jit_solution(12555607663916804609)
XLA Ops:
  0.6 16.7 %shard_map.76 = (bf16[1,128,2560]{2,1,0:T(8,128)(2,1)S(1)}, f32[128,256]{1,0:T(8,128)S(1)}, f32[128,256]{1,0:T(8,128)S(1)}) custom-call(bf16[1,128,2560]{2,1,0:T(8,128)(2,1)} %q_hbm.1, bf16[128,512]{1,0:T(8,128)(2,1)} %k_hbm.1, bf16[128,512]{1,0:T(8,128)(2,1)} %v_hbm.1, bf16[1,128,2560]{2,1,0:T(8,128)(2,1)} %g_hbm.1, s32[1,128]{1,0:T(1,128)} %bitcast.1), custom_call_target="tpu_custom_call" | custom-call | tf_op jit(solution)/shard_map/pallas_call | solution.py:529
  17.3 1.0 %shard_map.77 = (bf16[1,128,2560]{2,1,0:T(8,128)(2,1)}, f32[128,256]{1,0:T(8,128)}, f32[128,256]{1,0:T(8,128)}) custom-call(bf16[1,128,2560]{2,1,0:T(8,128)(2,1)S(1)} %get-tuple-element.6.dq_in, f32[128,256]{1,0:T(8,128)S(1)} %get-tuple-element.7.dk_in, f32[128,256]{1,0:T(8,128)S(1)} %get-tuple-element.8.dv_in), custom_call_target="tpu_custom_call" | custom-call | tf_op jit(solution)/shard_map/pallas_call | solution.py:564

commit v9 on v8

--- a/solution.py
+++ b/solution.py
@@ -435,8 +435,6 @@
 
             @pl.when(me >= step)
             def _(step=step):
-                if group == 0 and which == 0:
-                    near_seg[step].wait_recv()
                 near[step][group][which].wait_recv()
 
     query_send = [
@@ -453,10 +451,15 @@
             copy.wait_recv()
         own_products(1, group)
     far = slice(0, DOC_SHARDS * tok)
+    for step in steps:
+
+        @pl.when(me >= step)
+        def _(step=step):
+            near_seg[step].wait_recv()
+
+    fill_bias()
     for group in range(groups):
         near_arrived(group, 0)
-        if group == 0:
-            fill_bias()
         s_buf[group] = dot(k_buf[group, far, :], all_rows(q_buf, group), 1, 1)
         probabilities(group)
         send_part(group, 1, value_grads(far, group))

time: 18.4 us -> 18.4 us (level)
  no operation moved by 1% of the time
where the time goes in v9:
time: 18.4 us; the launch traced here: 18.3 us
  Pallas kernels  17.6 us (96%)
  between operations  0.64 us (3%)
    pallas_call x1, Pallas kernels, by_heads(): pl.pallas_call(functools.partial(kernel, cycle_size), out_shape=tuple((pl...  16.7 us
    pallas_call x1, Pallas kernels, by_heads(): pl.pallas_call(hand_over, out_shape=shapes, in_specs=[in_vmem] * 3, out_s...  0.97 us

profile of v9, /device:TPU:0, one launch (start us, length us, event | category | flops | bytes accessed | tf_op | source)
XLA Modules:
  0.0 18.3 jit_solution(13396552456065257965)
XLA Ops:
  0.6 16.7 %shard_map.76 = (bf16[1,128,2560]{2,1,0:T(8,128)(2,1)S(1)}, f32[128,256]{1,0:T(8,128)S(1)}, f32[128,256]{1,0:T(8,128)S(1)}) custom-call(bf16[1,128,2560]{2,1,0:T(8,128)(2,1)} %q_hbm.1, bf16[128,512]{1,0:T(8,128)(2,1)} %k_hbm.1, bf16[128,512]{1,0:T(8,128)(2,1)} %v_hbm.1, bf16[1,128,2560]{2,1,0:T(8,128)(2,1)} %g_hbm.1, s32[1,128]{1,0:T(1,128)} %bitcast.1), custom_call_target="tpu_custom_call" | custom-call | tf_op jit(solution)/shard_map/pallas_call | solution.py:532
  17.3 1.0 %shard_map.77 = (bf16[1,128,2560]{2,1,0:T(8,128)(2,1)}, f32[128,256]{1,0:T(8,128)}, f32[128,256]{1,0:T(8,128)}) custom-call(bf16[1,128,2560]{2,1,0:T(8,128)(2,1)S(1)} %get-tuple-element.6.dq_in, f32[128,256]{1,0:T(8,128)S(1)} %get-tuple-element.7.dk_in, f32[128,256]{1,0:T(8,128)S(1)} %get-tuple-element.8.dv_in), custom_call_target="tpu_custom_call" | custom-call | tf_op jit(solution)/shard_map/pallas_call | solution.py:567
